TPU v7x, 256 devices: a whole 4x4x8 slice. The times are simulated.
256 devices in a mesh: ctx: 64 (over z, x, y_lo), ch: 4 (over y_hi, core).
Axes of the slice: x: 4, y: 4 (y_hi: 2, y_lo: 2; y = y_hi * 2 + y_lo), z: 8, core: 2. Of those that a mesh axis runs over, the one named last changes fastest.
Arguments:
- inputs: float32 [4, 16384, 1024], P(None, 'ctx', 'ch'), may hold values from -6 to 6
- cotangent: float32 [4, 16384, 1024], P(None, 'ctx', 'ch'), may hold values from -6 to 6
- filters: float32 [16384, 1024], P('ctx', 'ch'), may hold values from -6 to 6
Outputs:
- input_grad: float32 [4, 16384, 1024], P(None, 'ctx', 'ch')
- filter_grad: float32 [16384, 1024], P('ctx', 'ch')
All inputs are finite; a program needn't handle non-finite values.
Results may differ from a plain program's by a relative error of at most 0.0001.
Values sent between devices are 32-bit elements; how exact they have to be, the bound alone decides.
No kernel may reach another device: no remote copies, remote signals or barrier semaphores. Data moves between devices by JAX's collectives and lax.ppermute only.
A program may use at most 128 MiB of HBM per device.

v0:
```python
import math

import jax
import jax.numpy as jnp
from jax import lax
from jax.sharding import PartitionSpec as P

HIGHEST = lax.Precision.HIGHEST


def swapped(value, axis, apart):
    mask = 2**apart
    pairs = [(source, source ^ mask) for source in range(lax.axis_size(axis))]
    return lax.ppermute(value, axis, pairs)


def spin(outer, inner, period):
    turns = outer[:, None] * inner[None, :] % period
    angle = turns.astype(jnp.float32) * (2.0 * math.pi / period)
    return (jnp.cos(angle), jnp.sin(angle))


def times_complex(left, right):
    return jnp.stack(
        [left[0] * right[0] - left[1] * right[1], left[0] * right[1] + left[1] * right[0]]
    )


def conjugate(value):
    return jnp.stack([value[0], -value[1]])


def channel_mirror(value):
    flipped = value[..., ::-1]
    for bit in range(lax.axis_size("ch").bit_length() - 1):
        flipped = swapped(flipped, "ch", bit)
    return flipped


def forward_transform(stacked):
    count = lax.axis_size("ctx")
    width = stacked.shape[1]
    block = width // count
    period = count * width
    here = lax.axis_index("ctx")
    pieces = lax.all_to_all(stacked[:, None], "ctx", split_axis=2, concat_axis=1, tiled=True)
    across = jnp.arange(count, dtype=jnp.int32)
    cos_n, sin_n = spin(across, across, count)
    real_part = jnp.einsum("pi,kijc->kpjc", cos_n, pieces, precision=HIGHEST)
    imag_part = -jnp.einsum("pi,kijc->kpjc", sin_n, pieces, precision=HIGHEST)
    local = here * block + jnp.arange(block, dtype=jnp.int32)
    cos_t, sin_t = spin(across, local, period)
    cos_t = cos_t[:, :, None]
    sin_t = sin_t[:, :, None]
    turned = jnp.stack(
        [real_part * cos_t + imag_part * sin_t, imag_part * cos_t - real_part * sin_t]
    )
    rows = jnp.arange(width, dtype=jnp.int32)
    cos_m, sin_m = spin(rows, rows, width)
    gathered = lax.all_to_all(turned, "ctx", split_axis=2, concat_axis=3, tiled=True)
    real_in = gathered[0, :, 0]
    imag_in = gathered[1, :, 0]
    real_out = jnp.einsum("mj,kjc->kmc", cos_m, real_in, precision=HIGHEST) + jnp.einsum(
        "mj,kjc->kmc", sin_m, imag_in, precision=HIGHEST
    )
    imag_out = jnp.einsum("mj,kjc->kmc", cos_m, imag_in, precision=HIGHEST) - jnp.einsum(
        "mj,kjc->kmc", sin_m, real_in, precision=HIGHEST
    )
    return jnp.stack([real_out, imag_out])


def inverse_transform(spectra):
    count = lax.axis_size("ctx")
    width = spectra.shape[2]
    period = count * width
    here = lax.axis_index("ctx")
    rows = jnp.arange(width, dtype=jnp.int32)
    cos_m, sin_m = spin(rows, rows, width)
    real_in = spectra[0]
    imag_in = spectra[1]
    real_part = jnp.einsum("jm,kmc->kjc", cos_m, real_in, precision=HIGHEST) - jnp.einsum(
        "jm,kmc->kjc", sin_m, imag_in, precision=HIGHEST
    )
    imag_part = jnp.einsum("jm,kmc->kjc", sin_m, real_in, precision=HIGHEST) + jnp.einsum(
        "jm,kmc->kjc", cos_m, imag_in, precision=HIGHEST
    )
    turns = rows * here % period
    angle = turns.astype(jnp.float32) * (2.0 * math.pi / period)
    cos_t = jnp.cos(angle)[None, :, None]
    sin_t = jnp.sin(angle)[None, :, None]
    turned = jnp.stack(
        [real_part * cos_t - imag_part * sin_t, real_part * sin_t + imag_part * cos_t]
    )[:, :, None]
    across = jnp.arange(count, dtype=jnp.int32)
    cos_n, sin_n = spin(across, across, count)
    gathered = lax.all_to_all(turned, "ctx", split_axis=3, concat_axis=2, tiled=True)
    blocks = jnp.einsum("iq,kqjc->kijc", cos_n, gathered[0], precision=HIGHEST) - jnp.einsum(
        "iq,kqjc->kijc", sin_n, gathered[1], precision=HIGHEST
    )
    merged = lax.all_to_all(blocks, "ctx", split_axis=1, concat_axis=2, tiled=True)
    return merged[:, 0]


def body(inputs, cotangent, filters):
    seqs = inputs.shape[0]
    width = inputs.shape[1]
    period = lax.axis_size("ctx") * width
    factor = 1.0 / (period * math.sqrt(2.0 * period))
    stacked = jnp.concatenate([inputs, cotangent, filters[None]], axis=0)
    spectra = forward_transform(stacked)
    data_spec = spectra[:, :seqs]
    grad_spec = spectra[:, seqs : 2 * seqs]
    filt_spec = spectra[:, 2 * seqs :]
    filt_back = channel_mirror(filt_spec)
    effective = filt_spec + conjugate(filt_back)
    input_spec = times_complex(conjugate(effective), grad_spec)
    cross = jnp.sum(times_complex(grad_spec, conjugate(data_spec)), axis=1, keepdims=True)
    cross = cross + conjugate(channel_mirror(cross))
    combined = jnp.concatenate([input_spec, cross], axis=1)
    grads = inverse_transform(combined) * factor
    return (grads[:seqs], grads[seqs])


def solution(mesh):
    in_specs = (P(None, "ctx", "ch"), P(None, "ctx", "ch"), P("ctx", "ch"))
    out_specs = (P(None, "ctx", "ch"), P("ctx", "ch"))
    return jax.shard_map(body, mesh=mesh, in_specs=in_specs, out_specs=out_specs, check_vma=False)
```

profile of v0, /device:TPU:1, one launch (start us, length us, event | category | flops | bytes accessed | tf_op | source)
XLA Modules:
  0.0 404.9 jit_solution(8934679546885623426)
XLA Ops:
  0.6 1.8 maximum_bitcast_fusion.1
  2.4 3.9 copy.66
  6.3 13.8 %all-to-all-start = ((f32[9,1,256,256]{3,1,0,2:T(1,128)}), f32[9,1,256,256]{3,1,0,2:T(1,128)S(1)}, u32[]{:S(2)}, u32[]{:S(2)}) async-start(f32[9,1,256,256]{3,1,0,2:T(1,128)} %copy.66), calls=%async_computation | async-start | bytes 4718592 | tf_op jit(solution)/shard_map/all_to_all | solution.py:46
  20.2 53.2 %all-to-all-done = f32[9,1,256,256]{3,1,0,2:T(1,128)S(1)} async-done(((f32[9,1,256,256]{3,1,0,2:T(1,128)}), f32[9,1,256,256]{3,1,0,2:T(1,128)S(1)}, u32[]{:S(2)}, u32[]{:S(2)}) %all-to-all-start) | async-done | bytes 2359328 | tf_op jit(solution)/shard_map/all_to_all | solution.py:46
  73.4 0.6 copy.98
  74.0 4.2 %fusion.8 = f32[9,4,256,64]{2,3,1,0:T(8,128)S(1)} fusion(f32[9,64,4,256]{3,0,2,1:T(8,128)S(1)} %bitcast.110), kind=kOutput, calls=%fused_computation.26 | convolution fusion | flops 453042176 | bytes 4718592 | tf_op jit(solution)/shard_map/pi,kijc->kpjc/dot_general | solution.py:50
  78.2 4.9 %fusion.1 = (f32[1,9,64,4,256]{4,2,3,1,0:T(8,128)S(1)}, f32[1,9,64,4,256]{4,2,3,1,0:T(8,128)S(1)}) fusion(f32[9,4,256,64]{2,3,1,0:T(8,128)S(1)} %fusion.8, f32[64,4]{0,1:T(4,128)S(1)} %get-tuple-element.29, f32[64,4]{0,1:T(4,128)S(1)} %get-tuple-element.28, f32[9,64,4,256]{3,0,2,1:T(8,128)S(1)} %bitcast.111), kind=kOutput, calls=%fused_computation.7 | convolution fusion | flops 457170944 | bytes 9439232 | tf_op jit(solution)/shard_map/pi,kijc->kpjc/dot_general | solution.py:49
  83.1 0.6 pad_maximum_fusion
  83.7 3.6 copy.70
  87.3 111.3 %all_to_all.19 = f32[2,9,64,4,256]{4,3,1,0,2:T(4,128)S(1)} all-to-all(f32[2,9,64,4,256]{4,3,1,0,2:T(4,128)S(1)} %copy.70), channel_id=1, replica_groups=mesh['ctx'=64,'ch'=4] {'ctx'}, dimensions={2} | all-to-all | bytes 9437184 | tf_op jit(solution)/shard_map/all_to_all | solution.py:60
  198.6 2.2 fusion.115
  200.8 1.9 copy.71
  202.7 2.7 squeeze.14
  205.4 6.1 %fusion.26 = f32[9,256,256]{2,1,0:T(8,128)} fusion(f32[9,256,256]{2,1,0:T(8,128)S(1)} %squeeze.14), kind=kOutput, calls=%fused_computation.60 | convolution fusion | flops 1812856832 | bytes 4718592 | tf_op jit(solution)/shard_map/mj,kjc->kmc/dot_general | solution.py:63
  211.5 1.9 copy.73
  213.4 3.7 squeeze.15
  217.2 6.6 %fusion.24 = f32[9,256,256]{2,1,0:T(8,128)S(1)} fusion(f32[9,256,256]{2,1,0:T(8,128)} %squeeze.15), kind=kOutput, calls=%fused_computation.58 | convolution fusion | flops 1812856832 | bytes 4718592 | tf_op jit(solution)/shard_map/mj,kjc->kmc/dot_general | solution.py:66
  223.9 4.9 %add_bitcast_fusion = f32[1,9,256,256]{2,3,1,0:T(8,128)S(1)} fusion(f32[9,256,256]{2,1,0:T(8,128)S(1)} %copy-done.5, f32[9,256,256]{2,1,0:T(8,128)S(1)} %copy-done), kind=kOutput, calls=%fused_computation.13 | convolution fusion | flops 1813446656 | bytes 7077888 | tf_op jit(solution)/shard_map/mj,kjc->kmc/dot_general | solution.py:63
  228.8 5.3 %subtract_bitcast_fusion = f32[1,9,256,256]{2,3,1,0:T(8,128)S(1)} fusion(f32[9,256,256]{2,1,0:T(8,128)S(1)} %fusion.24, f32[9,256,256]{2,1,0:T(8,128)S(1)} %squeeze.14), kind=kOutput, calls=%fused_computation.12 | convolution fusion | flops 1813446656 | bytes 7077888 | tf_op jit(solution)/shard_map/mj,kjc->kmc/dot_general | solution.py:66
  234.1 1.4 copy-done.3
  235.6 0.3 rev.6
  235.8 5.5 %collective-permute-start = (f32[2,1,256,256]{2,3,1,0:T(8,128)S(1)}, f32[2,1,256,256]{2,3,1,0:T(8,128)S(1)}, u32[]{:S(2)}, u32[]{:S(2)}) collective-permute-start(f32[2,1,256,256]{2,3,1,0:T(8,128)S(1)} %rev.6), channel_id=1, source_target_pairs={{0,1},{1,0},{2,3},{3,2},{4,5},{5,4},{6,7},{7,6},{8,9},{9,8},{10,11... | collective-permute-start | bytes 1572872 | tf_op jit(solution)/shard_map/ppermute | solution.py:14
  241.4 1.5 collective-permute-done
  242.9 2.6 collective-permute-start.1
  245.6 12.0 %collective-permute-done.1 = f32[2,1,256,256]{2,3,1,0:T(8,128)S(1)} collective-permute-done((f32[2,1,256,256]{2,3,1,0:T(8,128)S(1)}, f32[2,1,256,256]{2,3,1,0:T(8,128)S(1)}, u32[]{:S(2)}, u32[]{:S(2)}) %collective-permute-start.1) | collective-permute-done | bytes 524320 | tf_op jit(solution)/shard_map/ppermute | solution.py:14
  257.7 1.5 multiply_subtract_fusion.1
  259.4 0.3 reverse.3
  259.7 1.3 collective-permute-start.2
  261.0 1.5 collective-permute-done.2
  262.5 2.6 collective-permute-start.3
  265.2 12.0 %collective-permute-done.3 = f32[2,1,256,256]{2,3,1,0:T(8,128)S(1)} collective-permute-done((f32[2,1,256,256]{2,3,1,0:T(8,128)S(1)}, f32[2,1,256,256]{2,3,1,0:T(8,128)S(1)}, u32[]{:S(2)}, u32[]{:S(2)}) %collective-permute-start.3) | collective-permute-done | bytes 524320 | tf_op jit(solution)/shard_map/ppermute | solution.py:14
  277.3 0.3 pad_maximum_fusion.1
  277.6 2.2 fusion.13
  279.7 2.2 fusion.12
  281.9 2.2 convolution_subtract_fusion.1
  284.2 2.5 subtract_bitcast_fusion.1
  286.6 0.3 maximum_bitcast_fusion
  286.9 3.3 copy.78
  290.2 64.5 %all_to_all.40 = f32[2,5,1,256,256]{4,0,2,1,3:T(2,128)S(1)} all-to-all(f32[2,5,1,256,256]{4,0,2,1,3:T(2,128)} %copy.78), channel_id=1, replica_groups=mesh['ctx'=64,'ch'=4] {'ctx'}, dimensions={3} | all-to-all | bytes 5242880 | tf_op jit(solution)/shard_map/all_to_all | solution.py:96
  354.7 2.0 fusion.116
  357.0 2.2 fusion.6
  359.5 2.2 fusion.4
  361.7 0.8 copy.83
  362.6 39.2 %all_to_all.41 = f32[5,64,4,256]{3,2,0,1:T(4,128)S(1)} all-to-all(f32[5,64,4,256]{3,2,0,1:T(4,128)S(1)} %copy.83), channel_id=1, replica_groups=mesh['ctx'=64,'ch'=4] {'ctx'}, dimensions={1} | all-to-all | bytes 2621440 | tf_op jit(solution)/shard_map/all_to_all | solution.py:100
  401.8 0.3 broadcast_multiply_fusion
  402.1 0.3 slice.119
  402.7 1.2 copy.85
  403.9 0.8 squeeze.40
  (29 shorter events, 1.5 us)
Async XLA Ops:
  6.3 67.1 %all-to-all-start = ((f32[9,1,256,256]{3,1,0,2:T(1,128)}), f32[9,1,256,256]{3,1,0,2:T(1,128)S(1)}, u32[]{:S(2)}, u32[]{:S(2)}) async-start(f32[9,1,256,256]{3,1,0,2:T(1,128)} %copy.66), calls=%async_computation | async-start | bytes 4718592 | tf_op jit(solution)/shard_map/all_to_all | solution.py:46
  205.4 6.1 %copy-start.6 = (f32[1,9,64,4,256]{4,3,1,0,2:T(4,128)S(1)}, f32[1,9,64,4,256]{4,3,1,0,2:T(4,128)}, u32[]{:S(2)}) copy-start(f32[1,9,64,4,256]{4,3,1,0,2:T(4,128)} %get-tuple-element.16) | copy-start | bytes 7077892
  217.2 6.7 %copy-start = (f32[9,256,256]{2,1,0:T(8,128)S(1)}, f32[9,256,256]{2,1,0:T(8,128)}, u32[]{:S(2)}) copy-start(f32[9,256,256]{2,1,0:T(8,128)} %squeeze.15) | copy-start | bytes 7077892
  217.2 6.7 %copy-start.5 = (f32[9,256,256]{2,1,0:T(8,128)S(1)}, f32[9,256,256]{2,1,0:T(8,128)}, u32[]{:S(2)}) copy-start(f32[9,256,256]{2,1,0:T(8,128)} %fusion.26) | copy-start | bytes 7077892
  228.8 5.3 %copy-start.1 = (f32[1,9,256,256]{2,3,1,0:T(8,128)}, f32[1,9,256,256]{2,3,1,0:T(8,128)S(1)}, u32[]{:S(2)}) copy-start(f32[1,9,256,256]{2,3,1,0:T(8,128)S(1)} %add_bitcast_fusion) | copy-start | bytes 7077892
  234.1 1.4 copy-start.3
  235.5 22.2 %copy-start.2 = (f32[1,9,256,256]{2,3,1,0:T(8,128)S(1)}, f32[1,9,256,256]{2,3,1,0:T(8,128)}, u32[]{:S(2)}) copy-start(f32[1,9,256,256]{2,3,1,0:T(8,128)} %copy-done.1) | copy-start | bytes 7077892
  235.8 21.9 %copy-start.4 = (f32[1,9,256,256]{2,3,1,0:T(8,128)S(1)}, f32[1,9,256,256]{2,3,1,0:T(8,128)}, u32[]{:S(2)}) copy-start(f32[1,9,256,256]{2,3,1,0:T(8,128)} %copy-done.3) | copy-start | bytes 7077892
  235.8 7.1 %collective-permute-start = (f32[2,1,256,256]{2,3,1,0:T(8,128)S(1)}, f32[2,1,256,256]{2,3,1,0:T(8,128)S(1)}, u32[]{:S(2)}, u32[]{:S(2)}) collective-permute-start(f32[2,1,256,256]{2,3,1,0:T(8,128)S(1)} %rev.6), channel_id=1, source_target_pairs={{0,1},{1,0},{2,3},{3,2},{4,5},{5,4},{6,7},{7,6},{8,9},{9,8},{10,11... | collective-permute-start | bytes 1572872 | tf_op jit(solution)/shard_map/ppermute | solution.py:14
  242.9 14.6 %collective-permute-start.1 = (f32[2,1,256,256]{2,3,1,0:T(8,128)S(1)}, f32[2,1,256,256]{2,3,1,0:T(8,128)S(1)}, u32[]{:S(2)}, u32[]{:S(2)}) collective-permute-start(f32[2,1,256,256]{2,3,1,0:T(8,128)S(1)} %collective-permute-done), channel_id=1, source_target_pairs={{0,2},{1,3},{2,0},{3,1},{4,6},{5,7},{6,4},{7,5},{8,10},{9,11},{10,... | collective-permute-start | bytes 1572872 | tf_op jit(solution)/shard_map/ppermute | solution.py:14
  259.4 17.9 %copy-start.7 = (f32[1,4,256,256]{2,3,1,0:T(8,128)S(1)}, f32[1,4,256,256]{2,3,1,0:T(8,128)}, u32[]{:S(2)}) copy-start(f32[1,4,256,256]{2,3,1,0:T(8,128)} %get-tuple-element.11) | copy-start | bytes 3145732
  259.7 2.8 collective-permute-start.2
  262.5 14.6 %collective-permute-start.3 = (f32[2,1,256,256]{2,3,1,0:T(8,128)S(1)}, f32[2,1,256,256]{2,3,1,0:T(8,128)S(1)}, u32[]{:S(2)}, u32[]{:S(2)}) collective-permute-start(f32[2,1,256,256]{2,3,1,0:T(8,128)S(1)} %collective-permute-done.2), channel_id=1, source_target_pairs={{0,2},{1,3},{2,0},{3,1},{4,6},{5,7},{6,4},{7,5},{8,10},{9,11},{10,... | collective-permute-start | bytes 1572872 | tf_op jit(solution)/shard_map/ppermute | solution.py:14
where the time goes:
time: 411 us; the launch traced here: 405 us
  blocking collectives  215 us (52%)
  waiting for transfers between devices  80.2 us (20%)
  matrix products  45.6 us (11%)
  local copies, waits for them, and re-layouts  31.6 us (8%)
  starting transfers between devices  25.9 us (6%)
  other arithmetic  5.37 us (1%)
    all_to_all x1, blocking collectives, forward_transform(): lax.all_to_all(turned, 'ctx', split_axis=2, concat_axis=3, tiled=True)  111 us
    all_to_all x1, blocking collectives, inverse_transform(): lax.all_to_all(turned, 'ctx', split_axis=3, concat_axis=2, tiled=True)  64.5 us
    all_to_all x1, waiting for transfers between devices, forward_transform(): lax.all_to_all(stacked[:, None], 'ctx', split_axis=2, concat_axis=1, tile...  53.2 us
    all_to_all x1, blocking collectives, inverse_transform(): lax.all_to_all(blocks, 'ctx', split_axis=1, concat_axis=2, tiled=True)  39.2 us
    ppermute x4, waiting for transfers between devices, swapped(): return lax.ppermute(value, axis, pairs)  27 us
    all_to_all x1, starting transfers between devices, forward_transform(): lax.all_to_all(stacked[:, None], 'ctx', split_axis=2, concat_axis=1, tile...  13.8 us
    ppermute x4, starting transfers between devices, swapped(): return lax.ppermute(value, axis, pairs)  12.1 us
  transfers between devices with their start and end apart: 5, of which 5 were waited for; matrix products, arithmetic and copies ran while one was open for 0% of the time, Pallas kernels for 0%

commit v1 on v0

v1 whole, which is shorter than its diff:
```python
import functools
import math

import jax
import jax.numpy as jnp
import numpy as np
from jax import lax
from jax.experimental import pallas as pl
from jax.experimental.pallas import tpu as pltpu
from jax.sharding import PartitionSpec as P

BF = jnp.bfloat16
F32 = jnp.float32
ACROSS = 64
WIDTH = 256
PERIOD = ACROSS * WIDTH
HALF = 40
KEEP = ACROSS // 2 + 1
FACTOR = 1.0 / (PERIOD * math.sqrt(2.0 * PERIOD))
VMEM = 48 * 1024 * 1024


def two_parts(table):
    high = np.asarray(table, np.float32).astype(jnp.bfloat16)
    low = (table - high.astype(np.float64)).astype(np.float32).astype(jnp.bfloat16)
    return high, low


def tables():
    p = np.arange(HALF)
    i = np.arange(ACROSS)
    keep = (p < KEEP).astype(np.float64)
    angle = 2.0 * np.pi * (np.outer(p, i) % ACROSS) / ACROSS
    cos, sin = np.cos(angle) * keep[:, None], np.sin(angle) * keep[:, None]
    high, low = two_parts(np.concatenate([cos, -sin], 0))
    across = np.concatenate([high, low, high], 1)
    weight = np.where((p == 0) | (p == KEEP - 1), 1.0, 2.0) * keep * FACTOR
    back = np.concatenate([cos * weight[:, None], sin * weight[:, None]], 0).T
    high, low = two_parts(back)
    back = np.concatenate([high, low, high], 1)
    j = np.arange(WIDTH)
    turn = 2.0 * np.pi * np.outer(p, j) / PERIOD
    twiddle = np.stack([np.cos(turn), np.sin(turn)]).astype(np.float32)
    spin = 2.0 * np.pi * (np.outer(j, j) % WIDTH) / WIDTH
    c, s = np.cos(spin), np.sin(spin)
    high, low = two_parts(np.block([[c, -s], [s, c]]))
    return across, back, twiddle, high, low


def split(value):
    high = value.astype(BF)
    return high, (value - high.astype(F32)).astype(BF)


def dot(left, right):
    return jnp.dot(left, right, preferred_element_type=F32)


def placement():
    upper = lax.axis_index("ch") >= 2
    row = lax.broadcasted_iota(jnp.int32, (WIDTH, WIDTH), 0)
    column = lax.broadcasted_iota(jnp.int32, (WIDTH, WIDTH), 1)
    group = row % ACROSS
    group = jnp.where(upper, ACROSS - 1 - group, group)
    return jnp.where(column == row - row % ACROSS + group, 1.0, 0.0).astype(BF)


def pack_kernel(count, *refs):
    ins, out = refs[:-1], refs[-1]
    place = placement()
    rows = count * 8
    index = 0
    for ref in ins:
        for b in range(ref.shape[0]):
            value = ref[b]
            turned = jnp.zeros((WIDTH, WIDTH), F32)
            for part in split(value):
                turned = turned + lax.dot_general(
                    place, part, (((1,), (1,)), ((), ())), preferred_element_type=F32
                )
            for q in range(4):
                for half in range(2):
                    row = (index * 4 + q) * 2 + half
                    out[pl.ds(row, ACROSS, stride=rows), :] = turned[
                        q * ACROSS : (q + 1) * ACROSS, half * 128 : (half + 1) * 128
                    ]
            index += 1


def unpack_kernel(ref, out):
    place = placement()
    count = out.shape[0]
    rows = count * 8
    for b in range(count):
        pieces = []
        for q in range(4):
            halves = [
                ref[pl.ds((b * 4 + q) * 2 + half, ACROSS, stride=rows), :] for half in range(2)
            ]
            pieces.append(jnp.concatenate(halves, 1))
        value = jnp.concatenate(pieces, 0).T
        total = jnp.zeros((WIDTH, WIDTH), F32)
        for part in split(value):
            total = total + dot(part, place)
        out[b] = total


def load_pair(ref, rows, first):
    pieces = [ref[pl.ds(first * 2 + k, ACROSS, stride=rows), :] for k in range(4)]
    return jnp.concatenate(pieces, 1)


def spectra_of(load, count, across, twiddle, high_ref, low_ref, stage_hi, stage_lo, out, first):
    cos, sin = twiddle[0], twiddle[1]
    for pair in range(count // 2):
        high, low = split(load(pair * 2))
        part = dot(across[...], jnp.concatenate([high, high, low], 0))
        turned = []
        for k in range(2):
            re = part[:HALF, k * WIDTH : (k + 1) * WIDTH]
            im = part[HALF:, k * WIDTH : (k + 1) * WIDTH]
            turned.append(jnp.concatenate([re * cos + im * sin, im * cos - re * sin], 1))
        high, low = split(jnp.concatenate(turned, 0))
        stage_hi[pair * 80 : pair * 80 + 80] = high
        stage_lo[pair * 80 : pair * 80 + 80] = low
    size = count * HALF
    high, low = stage_hi[:size], stage_lo[:size]
    whole = dot(high, high_ref[...]) + (dot(low, high_ref[...]) + dot(high, low_ref[...]))
    out[first * HALF : first * HALF + size] = whole


def positions_of(spectra, count, back, twiddle, high_ref, low_ref, store):
    high, low = split(spectra)
    whole = dot(high, high_ref[...]) + (dot(low, high_ref[...]) + dot(high, low_ref[...]))
    cos, sin = twiddle[0], twiddle[1]
    for pair in range(count // 2):
        sides = []
        for k in range(2):
            piece = whole[(pair * 2 + k) * HALF : (pair * 2 + k + 1) * HALF]
            re, im = piece[:, :WIDTH], piece[:, WIDTH:]
            sides.append(jnp.concatenate([re * cos + im * sin, im * cos - re * sin], 0))
        high, low = split(jnp.concatenate(sides, 1))
        store(pair * 2, dot(back[...], jnp.concatenate([high, high, low], 0)))


def store_pair(ref, rows, first, value):
    for k in range(4):
        ref[pl.ds(first * 2 + k, ACROSS, stride=rows), :] = value[:, k * 128 : (k + 1) * 128]


def grads_kernel(got, mirrored, across, back, twiddle, high, low, out, kept, spec, stage_hi, stage_lo):
    spectra_of(lambda n: load_pair(got, 40, n), 20, across, twiddle, high, low, stage_hi, stage_lo, spec, 0)
    spectra_of(lambda n: load_pair(mirrored, 8, n), 4, across, twiddle, high, low, stage_hi, stage_lo, spec, 20)
    kept[...] = spec[: 16 * HALF]
    products = []
    for n in range(16):
        q = n % 4
        own = spec[(16 + q) * HALF : (17 + q) * HALF]
        other = spec[(20 + 3 - q) * HALF : (24 - q) * HALF]
        er = own[:, :WIDTH] + other[:, :WIDTH]
        ei = own[:, WIDTH:] - other[:, WIDTH:]
        cot = spec[n * HALF : (n + 1) * HALF]
        cr, ci = cot[:, :WIDTH], cot[:, WIDTH:]
        products.append(jnp.concatenate([er * cr + ei * ci, ei * cr - er * ci], 1))
    positions_of(
        jnp.concatenate(products, 0), 16, back, twiddle, high, low, functools.partial(store_pair, out, 32)
    )


def cross_kernel(got, kept, across, twiddle, high, low, out, spec, stage_hi, stage_lo):
    spectra_of(lambda n: load_pair(got, 32, n), 16, across, twiddle, high, low, stage_hi, stage_lo, spec, 0)
    for q in range(4):
        re = jnp.zeros((HALF, WIDTH), F32)
        im = jnp.zeros((HALF, WIDTH), F32)
        for b in range(4):
            n = b * 4 + q
            x, c = spec[n * HALF : (n + 1) * HALF], kept[n * HALF : (n + 1) * HALF]
            xr, xi, cr, ci = x[:, :WIDTH], x[:, WIDTH:], c[:, :WIDTH], c[:, WIDTH:]
            re = re + (cr * xr + ci * xi)
            im = im + (cr * xi - ci * xr)
        out[q * HALF : (q + 1) * HALF] = jnp.concatenate([re, im], 1)


def filter_kernel(own, other, back, twiddle, high, low, out):
    rows = []
    for q in range(4):
        a = own[q * HALF : (q + 1) * HALF]
        b = other[(3 - q) * HALF : (4 - q) * HALF]
        rows.append(jnp.concatenate([a[:, :WIDTH] + b[:, :WIDTH], a[:, WIDTH:] - b[:, WIDTH:]], 1))
    positions_of(
        jnp.concatenate(rows, 0), 4, back, twiddle, high, low, functools.partial(store_pair, out, 8)
    )


def call(kernel, shapes, scratch, flops, *args):
    moved = sum(a.size * a.dtype.itemsize for a in args) + sum(4 * math.prod(s) for s in shapes)
    out = pl.pallas_call(
        kernel,
        out_shape=[jax.ShapeDtypeStruct(s, F32) for s in shapes],
        scratch_shapes=scratch,
        compiler_params=pltpu.CompilerParams(vmem_limit_bytes=VMEM),
        cost_estimate=pl.CostEstimate(flops=flops, bytes_accessed=moved, transcendentals=0),
    )(*args)
    return out[0] if len(shapes) == 1 else out


def swap(value):
    return lax.ppermute(value, "ch", [(s, 3 - s) for s in range(4)])


def exchange(value):
    blocks = value.reshape(ACROSS, -1, 128)
    return lax.all_to_all(blocks, "ctx", 0, 0, tiled=True).reshape(-1, 128)


def body(inputs, cotangent, filters):
    across, back, twiddle, high, low = [jnp.asarray(t) for t in tables()]
    filters = filters[None]
    stages = [pltpu.VMEM((20 * HALF, 2 * WIDTH), BF)] * 2
    first = call(functools.partial(pack_kernel, 5), [(ACROSS * 40, 128)], [], 10**9, cotangent, filters)
    second = call(functools.partial(pack_kernel, 4), [(ACROSS * 32, 128)], [], 10**9, inputs)
    first = exchange(first)
    second = exchange(second)
    mirrored = swap(first.reshape(ACROSS, 40, 128)[:, 32:].reshape(ACROSS * 8, 128))
    grads, kept = call(
        grads_kernel,
        [(ACROSS * 32, 128), (16 * HALF, 2 * WIDTH)],
        [pltpu.VMEM((24 * HALF, 2 * WIDTH), F32)] + stages,
        5 * 10**9,
        first, mirrored, across, back, twiddle, high, low,
    )
    cross = call(
        cross_kernel,
        [(4 * HALF, 2 * WIDTH)],
        [pltpu.VMEM((16 * HALF, 2 * WIDTH), F32)] + stages,
        2 * 10**9,
        second, kept, across, twiddle, high, low,
    )
    filter_grad = call(
        filter_kernel, [(ACROSS * 8, 128)], [], 10**9, cross, swap(cross), back, twiddle, high, low
    )
    input_grad = call(unpack_kernel, [(4, WIDTH, WIDTH)], [], 10**9, exchange(grads))
    filter_grad = call(unpack_kernel, [(1, WIDTH, WIDTH)], [], 10**9, exchange(filter_grad))
    return (input_grad, filter_grad[0])


def solution(mesh):
    in_specs = (P(None, "ctx", "ch"), P(None, "ctx", "ch"), P("ctx", "ch"))
    out_specs = (P(None, "ctx", "ch"), P("ctx", "ch"))
    return jax.shard_map(body, mesh=mesh, in_specs=in_specs, out_specs=out_specs, check_vma=False)
```

time: 411 us -> 156 us (0.38)
  blocking collectives: 215 us -> 16 us
  matrix products: 45.6 us -> 0 us
  local copies, waits for them, and re-layouts: 31.6 us -> 5.37 us
  Pallas kernels: 0 us -> 14.3 us
  starting transfers between devices: 25.9 us -> 39.1 us
  other arithmetic: 5.37 us -> 0 us
    all_to_all x3 -> x1, blocking collectives: 215 us -> 16 us  [exchange(): return lax.all_to_all(blocks, 'ctx', 0, 0, tiled=True).reshape(-1, 128)]
    dot_general x12 -> x0, matrix products: 45.6 us -> none  [the longest x1 6.65 us: forward_transform(): jnp.einsum('mj,kjc->kmc', cos_m, imag_in, precision=HIGHEST)]
    all_to_all x1 -> x3, starting transfers between devices: 13.8 us -> 28.1 us  [exchange(): return lax.all_to_all(blocks, 'ctx', 0, 0, tiled=True).reshape(-1, 128)]
    pallas_call x0 -> x7, Pallas kernels: none -> 14.3 us  [call(): pl.pallas_call(kernel, out_shape=[jax.ShapeDtypeStruct(s, F32) for s in s...]
    slice x7 -> x0, local copies, waits for them, and re-layouts: 8.67 us -> none  [the longest x2 4.14 us: forward_transform(): imag_in = gathered[1, :, 0]]
    squeeze x3 -> x0, local copies, waits for them, and re-layouts: 7.16 us -> none  [the longest x1 3.7 us: forward_transform(): imag_in = gathered[1, :, 0]]
    broadcast_in_dim x2 -> x0, local copies, waits for them, and re-layouts: 7.12 us -> none  [the longest x1 3.86 us: forward_transform(): stacked[:, None]]
    ppermute x4 -> x2, waiting for transfers between devices: 27 us -> 20.6 us  [swap(): return lax.ppermute(value, 'ch', [(s, 3 - s) for s in range(4)])]
  transfers between devices with their start and end apart: 5 -> 5, of which waited for: 5 -> 5; matrix products, arithmetic and copies ran while one was open for 0% -> 0% of each run, Pallas kernels for 0% -> 5%
where the time goes in v1:
time: 156 us; the launch traced here: 153 us
  waiting for transfers between devices  77.7 us (50%)
  starting transfers between devices  39.1 us (25%)
  blocking collectives  16 us (10%)
  Pallas kernels  14.3 us (9%)
  local copies, waits for them, and re-layouts  5.37 us (3%)
    all_to_all x3, waiting for transfers between devices, exchange(): return lax.all_to_all(blocks, 'ctx', 0, 0, tiled=True).reshape(-1, 128)  57.1 us
    all_to_all x3, starting transfers between devices, exchange(): return lax.all_to_all(blocks, 'ctx', 0, 0, tiled=True).reshape(-1, 128)  28.1 us
    ppermute x2, waiting for transfers between devices, swap(): return lax.ppermute(value, 'ch', [(s, 3 - s) for s in range(4)])  20.6 us
    all_to_all x1, blocking collectives, exchange(): return lax.all_to_all(blocks, 'ctx', 0, 0, tiled=True).reshape(-1, 128)  16 us
    pallas_call x7, Pallas kernels, call(): pl.pallas_call(kernel, out_shape=[jax.ShapeDtypeStruct(s, F32) for s in s...  14.3 us
    ppermute x2, starting transfers between devices, swap(): return lax.ppermute(value, 'ch', [(s, 3 - s) for s in range(4)])  11 us
    unnamed x22, local copies, waits for them, and re-layouts  5.35 us
  transfers between devices with their start and end apart: 5, of which 5 were waited for; matrix products, arithmetic and copies ran while one was open for 0% of the time, Pallas kernels for 5%

profile of v1, /device:TPU:1, one launch (start us, length us, event | category | flops | bytes accessed | tf_op | source)
XLA Modules:
  0.0 153.2 jit_solution(4909470542628919199)
XLA Ops:
  0.6 0.0 copy-start
  0.6 1.2 copy-done
  1.9 0.0 copy-start.2
  1.9 0.9 copy-done.2
  2.8 1.7 %shard_map.95 = f32[2560,128]{1,0:T(8,128)} custom-call(f32[4,256,256]{2,1,0:T(8,128)S(1)} %copy-done, f32[1,256,256]{2,1,0:T(8,128)S(1)} %bitcast.17), custom_call_target="tpu_custom_call" | custom-call | flops 1000000000 | bytes 2621440 | tf_op jit(solution)/shard_map/pallas_call | solution.py:197
  4.5 0.0 copy-start.1
  4.5 13.6 %all-to-all-start = ((f32[64,40,128]{2,1,0:T(8,128)}), f32[64,40,128]{2,1,0:T(8,128)S(1)}, u32[]{:S(2)}, u32[]{:S(2)}) async-start(f32[64,40,128]{2,1,0:T(8,128)} %bitcast.1), calls=%async_computation | async-start | bytes 2621440 | tf_op jit(solution)/shard_map/all_to_all | solution.py:213
  18.1 0.0 copy-done.1
  18.1 1.9 %shard_map.98 = f32[2048,128]{1,0:T(8,128)} custom-call(f32[4,256,256]{2,1,0:T(8,128)S(1)} %copy-done.1), custom_call_target="tpu_custom_call" | custom-call | flops 1000000000 | bytes 2097152 | tf_op jit(solution)/shard_map/pallas_call | solution.py:197
  20.0 29.9 %all-to-all-done = f32[64,40,128]{2,1,0:T(8,128)S(1)} async-done(((f32[64,40,128]{2,1,0:T(8,128)}), f32[64,40,128]{2,1,0:T(8,128)S(1)}, u32[]{:S(2)}, u32[]{:S(2)}) %all-to-all-start) | async-done | bytes 1310752 | tf_op jit(solution)/shard_map/all_to_all | solution.py:213
  49.9 0.0 copy-start.3
  49.9 0.0 copy-start.4
  49.9 0.0 copy-start.5
  49.9 0.0 copy-start.6
  49.9 8.0 %all-to-all-start.2 = ((f32[64,32,128]{2,1,0:T(8,128)}), f32[64,32,128]{2,1,0:T(8,128)S(1)}, u32[]{:S(2)}, u32[]{:S(2)}) async-start(f32[64,32,128]{2,1,0:T(8,128)} %bitcast.6), calls=%async_computation.2 | async-start | bytes 2097152 | tf_op jit(solution)/shard_map/all_to_all | solution.py:213
  58.0 4.2 %collective-permute-start = (f32[512,128]{1,0:T(8,128)S(1)}, f32[512,128]{1,0:T(8,128)S(1)}, u32[]{:S(2)}, u32[]{:S(2)}) collective-permute-start(f32[512,128]{1,0:T(8,128)S(1)} %slice_bitcast_fusion), channel_id=1, source_target_pairs={{0,3},{1,2},{2,1},{3,0},{4,7},{5,6},{6,5},{7,4},{8,11},{9,10},{10,... | collective-permute-start | bytes 786440 | tf_op jit(solution)/shard_map/ppermute | solution.py:208
  62.2 12.1 %collective-permute-done.mirrored = f32[512,128]{1,0:T(8,128)S(1)} collective-permute-done((f32[512,128]{1,0:T(8,128)S(1)}, f32[512,128]{1,0:T(8,128)S(1)}, u32[]{:S(2)}, u32[]{:S(2)}) %collective-permute-start) | collective-permute-done | bytes 262176 | tf_op jit(solution)/shard_map/ppermute | solution.py:208
  74.3 0.0 copy-done.3
  74.3 0.0 copy-done.4
  74.3 0.0 copy-done.5
  74.4 0.0 copy-done.6
  74.4 0.0 copy-start.7
  74.4 0.7 copy-done.7
  75.1 5.3 %shard_map.96 = (f32[2048,128]{1,0:T(8,128)}, f32[640,512]{1,0:T(8,128)S(1)}) custom-call(f32[2560,128]{1,0:T(8,128)S(1)} %bitcast.12, f32[512,128]{1,0:T(8,128)S(1)} %collective-permute-done.mirrored, bf16[80,192]{1,0:T(8,128)(2,1)S(1)} %copy-done.6, bf16[64,240]{1,0:T(8,128)(2,1)S(1)} %copy-done.7, f32[2,40,256]{2,1,0:T(8,128)S(1)} %copy-done.5, ...), custom_call_target="tpu_custom_call" | custom-call | flops 5000000000 | bytes 5124096 | tf_op jit(solution)/shard_map/pallas_call | solution.py:197
  80.4 0.0 copy-start.9
  80.4 1.1 copy-done.9
  81.5 2.3 %all-to-all-done.2 = f32[64,32,128]{2,1,0:T(8,128)S(1)} async-done(((f32[64,32,128]{2,1,0:T(8,128)}), f32[64,32,128]{2,1,0:T(8,128)S(1)}, u32[]{:S(2)}, u32[]{:S(2)}) %all-to-all-start.2) | async-done | bytes 1048608 | tf_op jit(solution)/shard_map/all_to_all | solution.py:213
  83.8 0.0 copy-start.10
  83.8 1.3 copy-done.10
  85.1 0.0 copy-start.8
  85.1 1.9 %shard_map.99.own = f32[160,512]{1,0:T(8,128)S(1)} custom-call(f32[2048,128]{1,0:T(8,128)S(1)} %bitcast.13, f32[640,512]{1,0:T(8,128)S(1)} %copy-done.10, bf16[80,192]{1,0:T(8,128)(2,1)S(1)} %copy-done.6, f32[2,40,256]{2,1,0:T(8,128)S(1)} %copy-done.5, bf16[512,512]{1,0:T(8,128)(2,1)S(1)} %copy-done.3, bf16[512,512]{1,0:T(8,128)(2,1)S(1)} %copy-done.4), custom_call_target="tpu_custom_call" | custom-call | flops 2000000000 | bytes 3848192 | tf_op jit(solution)/shard_map/pallas_call | solution.py:197
  87.1 6.8 %collective-permute-start.1 = (f32[160,512]{1,0:T(8,128)S(1)}, f32[160,512]{1,0:T(8,128)S(1)}, u32[]{:S(2)}, u32[]{:S(2)}) collective-permute-start(f32[160,512]{1,0:T(8,128)S(1)} %shard_map.99.own), channel_id=1, source_target_pairs={{0,3},{1,2},{2,1},{3,0},{4,7},{5,6},{6,5},{7,4},{8,11},{9,10},{10,... | collective-permute-start | bytes 983048 | tf_op jit(solution)/shard_map/ppermute | solution.py:208
  93.9 8.5 %collective-permute-done.1.other = f32[160,512]{1,0:T(8,128)S(1)} collective-permute-done((f32[160,512]{1,0:T(8,128)S(1)}, f32[160,512]{1,0:T(8,128)S(1)}, u32[]{:S(2)}, u32[]{:S(2)}) %collective-permute-start.1) | collective-permute-done | bytes 327712 | tf_op jit(solution)/shard_map/ppermute | solution.py:208
  102.4 0.0 copy-done.8
  102.4 0.6 shard_map.100
  103.0 16.0 %all_to_all.20 = f32[64,8,128]{2,1,0:T(8,128)S(1)} all-to-all(f32[64,8,128]{2,1,0:T(8,128)S(1)} %bitcast.16), channel_id=1, replica_groups=mesh['ctx'=64,'ch'=4] {'ctx'}, dimensions={0} | all-to-all | bytes 524288 | tf_op jit(solution)/shard_map/all_to_all | solution.py:213
  119.0 6.5 %all-to-all-start.1 = ((f32[64,32,128]{2,1,0:T(8,128)}), f32[64,32,128]{2,1,0:T(8,128)S(1)}, u32[]{:S(2)}, u32[]{:S(2)}) async-start(f32[64,32,128]{2,1,0:T(8,128)} %bitcast.4), calls=%async_computation.1 | async-start | bytes 2097152 | tf_op jit(solution)/shard_map/all_to_all | solution.py:213
  125.5 1.0 shard_map.101
  126.5 24.9 %all-to-all-done.1 = f32[64,32,128]{2,1,0:T(8,128)S(1)} async-done(((f32[64,32,128]{2,1,0:T(8,128)}), f32[64,32,128]{2,1,0:T(8,128)S(1)}, u32[]{:S(2)}, u32[]{:S(2)}) %all-to-all-start.1) | async-done | bytes 1048608 | tf_op jit(solution)/shard_map/all_to_all | solution.py:213
  151.3 1.9 %shard_map.97 = f32[4,256,256]{2,1,0:T(8,128)} custom-call(f32[2048,128]{1,0:T(8,128)S(1)} %bitcast.14), custom_call_target="tpu_custom_call" | custom-call | flops 1000000000 | bytes 2097152 | tf_op jit(solution)/shard_map/pallas_call | solution.py:197
  (1 shorter events, 0.0 us)
Async XLA Ops:
  0.6 1.2 copy-start
  1.9 0.9 copy-start.2
  4.5 13.6 %copy-start.1 = (f32[4,256,256]{2,1,0:T(8,128)S(1)}, f32[4,256,256]{2,1,0:T(8,128)}, u32[]{:S(2)}) copy-start(f32[4,256,256]{2,1,0:T(8,128)} %refs_0_.3) | copy-start | bytes 3145732
  4.5 45.4 %all-to-all-start = ((f32[64,40,128]{2,1,0:T(8,128)}), f32[64,40,128]{2,1,0:T(8,128)S(1)}, u32[]{:S(2)}, u32[]{:S(2)}) async-start(f32[64,40,128]{2,1,0:T(8,128)} %bitcast.1), calls=%async_computation | async-start | bytes 2621440 | tf_op jit(solution)/shard_map/all_to_all | solution.py:213
  49.9 24.4 %copy-start.3 = (bf16[512,512]{1,0:T(8,128)(2,1)S(1)}, bf16[512,512]{1,0:T(8,128)(2,1)}, u32[]{:S(2)}) copy-start(bf16[512,512]{1,0:T(8,128)(2,1)} %constant.13.clone.high) | copy-start | bytes 1572868
  49.9 24.4 %copy-start.4 = (bf16[512,512]{1,0:T(8,128)(2,1)S(1)}, bf16[512,512]{1,0:T(8,128)(2,1)}, u32[]{:S(2)}) copy-start(bf16[512,512]{1,0:T(8,128)(2,1)} %constant.14.clone.low) | copy-start | bytes 1572868
  49.9 24.5 %copy-start.5 = (f32[2,40,256]{2,1,0:T(8,128)S(1)}, f32[2,40,256]{2,1,0:T(8,128)}, u32[]{:S(2)}) copy-start(f32[2,40,256]{2,1,0:T(8,128)} %constant.12.clone.twiddle) | copy-start | bytes 245764
  49.9 24.5 %copy-start.6 = (bf16[80,192]{1,0:T(8,128)(2,1)S(1)}, bf16[80,192]{1,0:T(8,128)(2,1)}, u32[]{:S(2)}) copy-start(bf16[80,192]{1,0:T(8,128)(2,1)} %constant.10.clone.across) | copy-start | bytes 92164
  49.9 33.9 %all-to-all-start.2 = ((f32[64,32,128]{2,1,0:T(8,128)}), f32[64,32,128]{2,1,0:T(8,128)S(1)}, u32[]{:S(2)}, u32[]{:S(2)}) async-start(f32[64,32,128]{2,1,0:T(8,128)} %bitcast.6), calls=%async_computation.2 | async-start | bytes 2097152 | tf_op jit(solution)/shard_map/all_to_all | solution.py:213
  58.0 16.4 %collective-permute-start = (f32[512,128]{1,0:T(8,128)S(1)}, f32[512,128]{1,0:T(8,128)S(1)}, u32[]{:S(2)}, u32[]{:S(2)}) collective-permute-start(f32[512,128]{1,0:T(8,128)S(1)} %slice_bitcast_fusion), channel_id=1, source_target_pairs={{0,3},{1,2},{2,1},{3,0},{4,7},{5,6},{6,5},{7,4},{8,11},{9,10},{10,... | collective-permute-start | bytes 786440 | tf_op jit(solution)/shard_map/ppermute | solution.py:208
  74.4 0.8 copy-start.7
  80.4 1.1 copy-start.9
  83.8 1.3 copy-start.10
  85.1 17.3 %copy-start.8 = (bf16[64,240]{1,0:T(8,128)(2,1)S(1)}, bf16[64,240]{1,0:T(8,128)(2,1)}, u32[]{:S(2)}) copy-start(bf16[64,240]{1,0:T(8,128)(2,1)} %constant.11.clone.back) | copy-start | bytes 92164
  87.1 15.3 %collective-permute-start.1 = (f32[160,512]{1,0:T(8,128)S(1)}, f32[160,512]{1,0:T(8,128)S(1)}, u32[]{:S(2)}, u32[]{:S(2)}) collective-permute-start(f32[160,512]{1,0:T(8,128)S(1)} %shard_map.99.own), channel_id=1, source_target_pairs={{0,3},{1,2},{2,1},{3,0},{4,7},{5,6},{6,5},{7,4},{8,11},{9,10},{10,... | collective-permute-start | bytes 983048 | tf_op jit(solution)/shard_map/ppermute | solution.py:208
  119.0 32.3 %all-to-all-start.1 = ((f32[64,32,128]{2,1,0:T(8,128)}), f32[64,32,128]{2,1,0:T(8,128)S(1)}, u32[]{:S(2)}, u32[]{:S(2)}) async-start(f32[64,32,128]{2,1,0:T(8,128)} %bitcast.4), calls=%async_computation.1 | async-start | bytes 2097152 | tf_op jit(solution)/shard_map/all_to_all | solution.py:213

commit v2 on v1

v2 whole, which is shorter than its diff:
```python
import functools
import math

import jax
import jax.numpy as jnp
import numpy as np
from jax import lax
from jax.experimental import pallas as pl
from jax.experimental.pallas import tpu as pltpu
from jax.sharding import PartitionSpec as P

BF = jnp.bfloat16
F32 = jnp.float32
ACROSS = 64
DEVICES = 256
WIDTH = 256
PERIOD = ACROSS * WIDTH
HALF = 40
KEEP = ACROSS // 2 + 1
FACTOR = 1.0 / (PERIOD * math.sqrt(2.0 * PERIOD))
VMEM = 48 * 1024 * 1024


def two_parts(table):
    high = np.asarray(table, np.float32).astype(jnp.bfloat16)
    low = (table - high.astype(np.float64)).astype(np.float32).astype(jnp.bfloat16)
    return high, low


def tables():
    p = np.arange(HALF)
    i = np.arange(ACROSS)
    keep = (p < KEEP).astype(np.float64)
    angle = 2.0 * np.pi * (np.outer(p, i) % ACROSS) / ACROSS
    cos, sin = np.cos(angle) * keep[:, None], np.sin(angle) * keep[:, None]
    high, low = two_parts(np.concatenate([cos, -sin], 0))
    across = np.concatenate([high, low, high], 1)
    weight = np.where((p == 0) | (p == KEEP - 1), 1.0, 2.0) * keep * FACTOR
    back = np.concatenate([cos * weight[:, None], sin * weight[:, None]], 0).T
    high, low = two_parts(back)
    back = np.concatenate([high, low, high], 1)
    j = np.arange(WIDTH)
    turn = 2.0 * np.pi * np.outer(p, j) / PERIOD
    twiddle = np.stack([np.cos(turn), np.sin(turn)]).astype(np.float32)
    spin = 2.0 * np.pi * (np.outer(j, j) % WIDTH) / WIDTH
    c, s = np.cos(spin), np.sin(spin)
    high, low = two_parts(np.block([[c, -s], [s, c]]))
    return across, back, twiddle, high, low


def split(value):
    high = value.astype(BF)
    return high, (value - high.astype(F32)).astype(BF)


def dot(left, right):
    return jnp.dot(left, right, preferred_element_type=F32)


def placement():
    upper = lax.axis_index("ch") >= 2
    row = lax.broadcasted_iota(jnp.int32, (WIDTH, WIDTH), 0)
    column = lax.broadcasted_iota(jnp.int32, (WIDTH, WIDTH), 1)
    return jnp.where(column == jnp.where(upper, WIDTH - 1 - row, row), 1.0, 0.0).astype(BF)


def pack_kernel(cotangent, filters, inputs, out, held, sems):
    blocks = [cotangent.at[b] for b in range(4)] + [filters] + [inputs.at[b] for b in range(4)]
    copies = [pltpu.make_async_copy(block, held.at[u], sems.at[u]) for u, block in enumerate(blocks)]
    for copy in copies:
        copy.start()
    place = placement()
    for u, copy in enumerate(copies):
        copy.wait()
        turned = jnp.zeros((WIDTH, WIDTH), F32)
        for part in split(held[u]):
            turned = turned + lax.dot_general(
                place, part, (((1,), (1,)), ((), ())), preferred_element_type=F32
            )
        for half in range(2):
            out[pl.ds(u * 2 + half, DEVICES, stride=18), :] = turned[:, half * 128 : (half + 1) * 128]


def unpack_kernel(ref, inputs, filters, held, sems):
    place = placement()
    blocks = [inputs.at[b] for b in range(4)] + [filters]
    copies = []
    for u, block in enumerate(blocks):
        halves = [ref[pl.ds(u * 2 + half, DEVICES, stride=10), :] for half in range(2)]
        value = jnp.concatenate(halves, 1).T
        total = jnp.zeros((WIDTH, WIDTH), F32)
        for part in split(value):
            total = total + dot(part, place)
        held[u] = total
        copies.append(pltpu.make_async_copy(held.at[u], block, sems.at[u]))
        copies[-1].start()
    for copy in copies:
        copy.wait()


def load_pair(ref, first):
    pieces = []
    for n in (first, first + 1):
        for half in range(2):
            row = ((n % 4) * 9 + n // 4) * 2 + half
            pieces.append(ref[pl.ds(row, ACROSS, stride=72), :])
    return jnp.concatenate(pieces, 1)


def spectra_of(load, count, across, twiddle, high_ref, low_ref, stage_hi, stage_lo, out, first):
    cos, sin = twiddle[0], twiddle[1]
    for pair in range(count // 2):
        high, low = split(load(pair * 2))
        part = dot(across[...], jnp.concatenate([high, high, low], 0))
        turned = []
        for k in range(2):
            re = part[:HALF, k * WIDTH : (k + 1) * WIDTH]
            im = part[HALF:, k * WIDTH : (k + 1) * WIDTH]
            turned.append(jnp.concatenate([re * cos + im * sin, im * cos - re * sin], 1))
        high, low = split(jnp.concatenate(turned, 0))
        stage_hi[pair * 80 : pair * 80 + 80] = high
        stage_lo[pair * 80 : pair * 80 + 80] = low
    size = count * HALF
    high, low = stage_hi[:size], stage_lo[:size]
    whole = dot(high, high_ref[...]) + (dot(low, high_ref[...]) + dot(high, low_ref[...]))
    out[first * HALF : first * HALF + size] = whole


def positions_of(spectra, count, back, twiddle, high_ref, low_ref, store):
    high, low = split(spectra)
    whole = dot(high, high_ref[...]) + (dot(low, high_ref[...]) + dot(high, low_ref[...]))
    cos, sin = twiddle[0], twiddle[1]
    for pair in range(count // 2):
        sides = []
        for k in range(2):
            piece = whole[(pair * 2 + k) * HALF : (pair * 2 + k + 1) * HALF]
            re, im = piece[:, :WIDTH], piece[:, WIDTH:]
            sides.append(jnp.concatenate([re * cos + im * sin, im * cos - re * sin], 0))
        high, low = split(jnp.concatenate(sides, 1))
        store(pair * 2, dot(back[...], jnp.concatenate([high, high, low], 0)))


def store_pair(ref, first, value):
    for k in range(4):
        n = first + k // 2
        row = ((n % 4) * 5 + n // 4) * 2 + k % 2
        ref[pl.ds(row, ACROSS, stride=40), :] = value[:, k * 128 : (k + 1) * 128]


def grads_kernel(got, across, back, twiddle, high, low, out, spec, stage_hi, stage_lo):
    load = functools.partial(load_pair, got)
    spectra_of(load, 36, across, twiddle, high, low, stage_hi, stage_lo, spec, 0)
    products = []
    for n in range(16):
        s = n % 4
        own = spec[(16 + s) * HALF : (17 + s) * HALF]
        other = spec[(19 - s) * HALF : (20 - s) * HALF]
        er = own[:, :WIDTH] + other[:, :WIDTH]
        ei = own[:, WIDTH:] - other[:, WIDTH:]
        cot = spec[n * HALF : (n + 1) * HALF]
        cr, ci = cot[:, :WIDTH], cot[:, WIDTH:]
        products.append(jnp.concatenate([er * cr + ei * ci, ei * cr - er * ci], 1))
    crosses = []
    for s in range(4):
        re = jnp.zeros((HALF, WIDTH), F32)
        im = jnp.zeros((HALF, WIDTH), F32)
        for b in range(4):
            n = b * 4 + s
            c, x = spec[n * HALF : (n + 1) * HALF], spec[(20 + n) * HALF : (21 + n) * HALF]
            xr, xi, cr, ci = x[:, :WIDTH], x[:, WIDTH:], c[:, :WIDTH], c[:, WIDTH:]
            re = re + (cr * xr + ci * xi)
            im = im + (cr * xi - ci * xr)
        crosses.append((re, im))
    for s in range(4):
        a, b = crosses[s], crosses[3 - s]
        products.append(jnp.concatenate([a[0] + b[0], a[1] - b[1]], 1))
    positions_of(
        jnp.concatenate(products, 0), 20, back, twiddle, high, low, functools.partial(store_pair, out)
    )


def call(kernel, outs, scratch, flops, *args, in_specs=None, out_specs=None):
    moved = sum(a.size * a.dtype.itemsize for a in args) + sum(4 * math.prod(o) for o in outs)
    options = dict(in_specs=in_specs) if in_specs else {}
    if out_specs:
        options["out_specs"] = out_specs
    return pl.pallas_call(
        kernel,
        out_shape=[jax.ShapeDtypeStruct(o, F32) for o in outs],
        scratch_shapes=scratch,
        compiler_params=pltpu.CompilerParams(vmem_limit_bytes=VMEM),
        cost_estimate=pl.CostEstimate(flops=flops, bytes_accessed=moved, transcendentals=0),
        **options,
    )(*args)


def exchange(value, units):
    blocks = value.reshape(DEVICES, units, 2, 128)
    return lax.all_to_all(blocks, ("ctx", "ch"), 0, 0, tiled=True).reshape(-1, 128)


def body(inputs, cotangent, filters):
    across, back, twiddle, high, low = [jnp.asarray(t) for t in tables()]
    anywhere = pl.BlockSpec(memory_space=pl.ANY)
    (packed,) = call(
        pack_kernel,
        [(DEVICES * 18, 128)],
        [pltpu.VMEM((9, WIDTH, WIDTH), F32), pltpu.SemaphoreType.DMA((9,))],
        10**9,
        cotangent, filters, inputs,
        in_specs=[anywhere] * 3,
    )
    got = exchange(packed, 9)
    (grads,) = call(
        grads_kernel,
        [(DEVICES * 10, 128)],
        [pltpu.VMEM((36 * HALF, 2 * WIDTH), F32)] + [pltpu.VMEM((36 * HALF, 2 * WIDTH), BF)] * 2,
        8 * 10**9,
        got, across, back, twiddle, high, low,
    )
    return tuple(
        call(
            unpack_kernel,
            [(4, WIDTH, WIDTH), (WIDTH, WIDTH)],
            [pltpu.VMEM((5, WIDTH, WIDTH), F32), pltpu.SemaphoreType.DMA((5,))],
            10**9,
            exchange(grads, 5),
            out_specs=[anywhere] * 2,
        )
    )


def solution(mesh):
    in_specs = (P(None, "ctx", "ch"), P(None, "ctx", "ch"), P("ctx", "ch"))
    out_specs = (P(None, "ctx", "ch"), P("ctx", "ch"))
    return jax.shard_map(body, mesh=mesh, in_specs=in_specs, out_specs=out_specs, check_vma=False)
```

time: 156 us -> 132 us (0.85); the launches traced: 153 us -> 132 us
  blocking collectives: 16 us -> 118 us
  waiting for transfers between devices: 77.7 us -> 0 us
  starting transfers between devices: 39.1 us -> 0 us
  Pallas kernels: 14.3 us -> 10.2 us
  local copies, waits for them, and re-layouts: 5.37 us -> 3.43 us
    all_to_all x1 -> x2, blocking collectives: 16 us -> 118 us  [exchange(): lax.all_to_all(blocks, ('ctx', 'ch'), 0, 0, tiled=True).reshape(-1, 128)]
    all_to_all x3 -> x0, waiting for transfers between devices: 57.1 us -> none  [exchange(): return lax.all_to_all(blocks, 'ctx', 0, 0, tiled=True).reshape(-1, 128)]
    all_to_all x3 -> x0, starting transfers between devices: 28.1 us -> none  [exchange(): return lax.all_to_all(blocks, 'ctx', 0, 0, tiled=True).reshape(-1, 128)]
    ppermute x2 -> x0, waiting for transfers between devices: 20.6 us -> none  [swap(): return lax.ppermute(value, 'ch', [(s, 3 - s) for s in range(4)])]
    ppermute x2 -> x0, starting transfers between devices: 11 us -> none  [swap(): return lax.ppermute(value, 'ch', [(s, 3 - s) for s in range(4)])]
    pallas_call x7 -> x3, Pallas kernels: 14.3 us -> 10.2 us  [call(): pl.pallas_call(kernel, out_shape=[jax.ShapeDtypeStruct(o, F32) for o in o...]
    unnamed x22 -> x16, local copies, waits for them, and re-layouts: 5.35 us -> 3.43 us
  transfers between devices with their start and end apart: 5 -> 0, of which waited for: 5 -> 0; matrix products, arithmetic and copies ran while one was open for 0% -> 0% of each run, Pallas kernels for 5% -> 0%
where the time goes in v2:
time: 132 us
  blocking collectives  118 us (89%)
  Pallas kernels  10.2 us (8%)
  local copies, waits for them, and re-layouts  3.43 us (3%)
    all_to_all x2, blocking collectives, exchange(): lax.all_to_all(blocks, ('ctx', 'ch'), 0, 0, tiled=True).reshape(-1, 128)  118 us
    pallas_call x3, Pallas kernels, call(): pl.pallas_call(kernel, out_shape=[jax.ShapeDtypeStruct(o, F32) for o in o...  10.2 us
    unnamed x16, local copies, waits for them, and re-layouts  3.43 us

profile of v2, /device:TPU:1, one launch (start us, length us, event | category | flops | bytes accessed | tf_op | source)
XLA Modules:
  0.0 131.9 jit_solution(9965062206388008605)
XLA Ops:
  0.6 0.0 copy-start
  0.6 1.2 copy-done
  1.9 0.0 copy-start.1
  1.9 1.2 copy-done.1
  3.1 0.0 copy-start.2
  3.1 0.9 copy-done.2
  4.0 3.1 %shard_map.95 = f32[4608,128]{1,0:T(8,128)S(1)} custom-call(f32[4,256,256]{2,1,0:T(8,128)S(1)} %copy-done, f32[256,256]{1,0:T(8,128)S(1)} %copy-done.2, f32[4,256,256]{2,1,0:T(8,128)S(1)} %copy-done.1), custom_call_target="tpu_custom_call" | custom-call | flops 1000000000 | bytes 4718592 | tf_op jit(solution)/shard_map/pallas_call | solution.py:187
  7.2 0.0 copy-start.3
  7.2 0.0 copy-start.4
  7.2 0.0 copy-start.5
  7.2 0.0 copy-start.6
  7.2 0.0 copy-start.7
  7.2 73.8 %all_to_all.10 = f32[256,9,2,128]{3,2,1,0:T(2,128)S(1)} all-to-all(f32[256,9,2,128]{3,2,1,0:T(2,128)S(1)} %bitcast.4), channel_id=1, replica_groups=mesh['ctx'=64,'ch'=4] {'ctx','ch'}, dimensions={0} | all-to-all | bytes 4718592 | tf_op jit(solution)/shard_map/all_to_all | solution.py:199
  81.0 0.0 copy-done.3
  81.0 0.0 copy-done.4
  81.0 0.0 copy-done.5
  81.0 0.0 copy-done.6
  81.0 0.0 copy-done.7
  81.1 5.6 %shard_map.96 = f32[2560,128]{1,0:T(8,128)S(1)} custom-call(f32[4608,128]{1,0:T(8,128)S(1)} %bitcast.5, bf16[80,192]{1,0:T(8,128)(2,1)S(1)} %copy-done.6, bf16[64,240]{1,0:T(8,128)(2,1)S(1)} %copy-done.7, f32[2,40,256]{2,1,0:T(8,128)S(1)} %copy-done.5, bf16[512,512]{1,0:T(8,128)(2,1)S(1)} %copy-done.4, bf16[512,512]{1,0:T(8,128)(2,1)S(1)} %copy-done.3), custom_call_target="tpu_custom_call" | custom-call | flops 8000000000 | bytes 4861952 | tf_op jit(solution)/shard_map/pallas_call | solution.py:187
  86.7 43.8 %all_to_all.11 = f32[256,5,2,128]{3,2,1,0:T(2,128)S(1)} all-to-all(f32[256,5,2,128]{3,2,1,0:T(2,128)S(1)} %bitcast.6), channel_id=1, replica_groups=mesh['ctx'=64,'ch'=4] {'ctx','ch'}, dimensions={0} | all-to-all | bytes 2621440 | tf_op jit(solution)/shard_map/all_to_all | solution.py:199
  130.5 1.5 %shard_map.97 = (f32[4,256,256]{2,1,0:T(8,128)}, f32[256,256]{1,0:T(8,128)}) custom-call(f32[2560,128]{1,0:T(8,128)S(1)} %bitcast.7), custom_call_target="tpu_custom_call" | custom-call | flops 1000000000 | bytes 2621440 | tf_op jit(solution)/shard_map/pallas_call | solution.py:187
Async XLA Ops:
  0.6 1.2 copy-start
  1.9 1.2 copy-start.1
  3.1 0.9 copy-start.2
  7.2 73.9 %copy-start.3 = (bf16[512,512]{1,0:T(8,128)(2,1)S(1)}, bf16[512,512]{1,0:T(8,128)(2,1)}, u32[]{:S(2)}) copy-start(bf16[512,512]{1,0:T(8,128)(2,1)} %constant.14.clone.low) | copy-start | bytes 1572868
  7.2 73.9 %copy-start.4 = (bf16[512,512]{1,0:T(8,128)(2,1)S(1)}, bf16[512,512]{1,0:T(8,128)(2,1)}, u32[]{:S(2)}) copy-start(bf16[512,512]{1,0:T(8,128)(2,1)} %constant.13.clone.high) | copy-start | bytes 1572868
  7.2 73.9 %copy-start.5 = (f32[2,40,256]{2,1,0:T(8,128)S(1)}, f32[2,40,256]{2,1,0:T(8,128)}, u32[]{:S(2)}) copy-start(f32[2,40,256]{2,1,0:T(8,128)} %constant.12.clone.twiddle) | copy-start | bytes 245764
  7.2 73.8 %copy-start.6 = (bf16[80,192]{1,0:T(8,128)(2,1)S(1)}, bf16[80,192]{1,0:T(8,128)(2,1)}, u32[]{:S(2)}) copy-start(bf16[80,192]{1,0:T(8,128)(2,1)} %constant.10.clone.across) | copy-start | bytes 92164
  7.2 73.8 %copy-start.7 = (bf16[64,240]{1,0:T(8,128)(2,1)S(1)}, bf16[64,240]{1,0:T(8,128)(2,1)}, u32[]{:S(2)}) copy-start(bf16[64,240]{1,0:T(8,128)(2,1)} %constant.11.clone.back) | copy-start | bytes 92164

commit v3 on v2

v3 whole, which is shorter than its diff:
```python
import functools
import math

import jax
import jax.numpy as jnp
import numpy as np
from jax import lax
from jax.experimental import pallas as pl
from jax.experimental.pallas import tpu as pltpu
from jax.sharding import PartitionSpec as P

BF = jnp.bfloat16
F32 = jnp.float32
ACROSS = 64
DEVICES = 256
WIDTH = 256
PERIOD = ACROSS * WIDTH
HALF = ACROSS // 2
FACTOR = 1.0 / (PERIOD * math.sqrt(2.0 * PERIOD))
VMEM = 48 * 1024 * 1024
PACK_VMEM = 56 * 1024 * 1024


def two_parts(table):
    high = np.asarray(table, np.float32).astype(jnp.bfloat16)
    low = (table - high.astype(np.float64)).astype(np.float32).astype(jnp.bfloat16)
    return high, low


def tables():
    p = np.arange(HALF)
    i = np.arange(ACROSS)
    angle = 2.0 * np.pi * (np.outer(p, i) % ACROSS) / ACROSS
    cos, sin = np.cos(angle), np.sin(angle)
    last = np.cos(np.pi * i)
    fore = np.concatenate([cos, -sin], 0)
    fore[HALF] = last
    high, low = two_parts(fore)
    across = np.concatenate([high, low, high], 1)
    weight = np.where(p == 0, 1.0, 2.0)[:, None] * FACTOR
    back = np.concatenate([cos * weight, sin * weight], 0)
    back[HALF] = last * FACTOR
    high, low = two_parts(back.T)
    back = np.concatenate([high, low, high], 1)
    j = np.arange(WIDTH)
    turn = 2.0 * np.pi * np.outer(np.arange(HALF + 1), j) / PERIOD
    c, s = np.cos(turn), np.sin(turn)
    masked = c[:HALF] * (p > 0)[:, None]
    ends = np.zeros((HALF, WIDTH))
    ends[0], ends[1] = c[HALF], s[HALF]
    twiddle = np.stack([c[:HALF], s[:HALF], masked, ends]).astype(np.float32)
    spin = 2.0 * np.pi * (np.outer(j, j) % WIDTH) / WIDTH
    c, s = np.cos(spin), np.sin(spin)
    high, low = two_parts(np.block([[c, -s], [s, c]]))
    return across, back, twiddle, np.concatenate([high, high, low], 0)


def split(value):
    high = value.astype(BF)
    return high, (value - high.astype(F32)).astype(BF)


def dot(left, right):
    return jnp.dot(left, right, preferred_element_type=F32)


def placement():
    upper = lax.axis_index("ch") >= 2
    row = lax.broadcasted_iota(jnp.int32, (WIDTH, WIDTH), 0)
    column = lax.broadcasted_iota(jnp.int32, (WIDTH, WIDTH), 1)
    return jnp.where(column == jnp.where(upper, WIDTH - 1 - row, row), 1.0, 0.0).astype(BF)


def pack_kernel(cotangent, filters, inputs, out, held, sems):
    blocks = [cotangent.at[b] for b in range(4)] + [filters] + [inputs.at[b] for b in range(4)]
    copies = [pltpu.make_async_copy(block, held.at[u], sems.at[u]) for u, block in enumerate(blocks)]
    for copy in copies:
        copy.start()
    place = placement()
    for u, copy in enumerate(copies):
        copy.wait()
        high, low = split(held[u])
        turned = (dot(high, place) + dot(low, place)).T
        for half in range(2):
            out[pl.ds(u * 2 + half, DEVICES, stride=18), :] = turned[:, half * 128 : (half + 1) * 128]


def unpack_kernel(ref, inputs, filters, held, sems):
    place = placement()
    blocks = [inputs.at[b] for b in range(4)] + [filters]
    copies = []
    for u, block in enumerate(blocks):
        halves = [ref[pl.ds(u * 2 + half, DEVICES, stride=10), :] for half in range(2)]
        value = jnp.concatenate(halves, 1).T
        total = jnp.zeros((WIDTH, WIDTH), F32)
        for part in split(value):
            total = total + dot(part, place)
        held[u] = total
        copies.append(pltpu.make_async_copy(held.at[u], block, sems.at[u]))
        copies[-1].start()
    for copy in copies:
        copy.wait()


def load_pair(ref, first):
    pieces = []
    for n in (first, first + 1):
        for half in range(2):
            row = ((n % 4) * 9 + n // 4) * 2 + half
            pieces.append(ref[pl.ds(row, ACROSS, stride=72), :])
    return jnp.concatenate(pieces, 1)


def spin_rows(high, low, table):
    return dot(jnp.concatenate([high, low, high], 1), table[...])


def spectra_of(load, count, across, twiddle, table, stage_hi, stage_lo, ends, spec):
    cos, sin, masked = twiddle[0], twiddle[1], twiddle[2]
    for pair in range(count // 2):
        high, low = split(load(pair * 2))
        part = dot(across[...], jnp.concatenate([high, high, low], 0))
        turned = []
        for k in range(2):
            re = part[:HALF, k * WIDTH : (k + 1) * WIDTH]
            im = part[HALF:, k * WIDTH : (k + 1) * WIDTH]
            ends[pair * 2 + k : pair * 2 + k + 1, :] = im[:1]
            turned.append(jnp.concatenate([re * cos + im * sin, im * masked - re * sin], 1))
        high, low = split(jnp.concatenate(turned, 0))
        stage_hi[pair * 64 : pair * 64 + 64] = high
        stage_lo[pair * 64 : pair * 64 + 64] = low
    base, more = count * HALF, ends.shape[0]
    last = ends[...]
    high, low = split(jnp.concatenate([last * twiddle[3, 0:1], -last * twiddle[3, 1:2]], 1))
    stage_hi[base : base + more] = high
    stage_lo[base : base + more] = low
    spec[...] = spin_rows(stage_hi[: base + more], stage_lo[: base + more], table)


def positions_of(count, back, twiddle, table, stage_hi, stage_lo, spec, store):
    base = count * HALF
    size = base + 32
    spec[:size] = spin_rows(stage_hi[:size], stage_lo[:size], table)
    cos, sin = twiddle[0], twiddle[1]
    first = lax.broadcasted_iota(jnp.int32, (8, WIDTH), 0) == 0
    ends = spec[base:size]
    ends = ends[:, :WIDTH] * twiddle[3, 0:1] + ends[:, WIDTH:] * twiddle[3, 1:2]
    for pair in range(count // 2):
        sides = []
        for k in range(2):
            n = pair * 2 + k
            piece = spec[n * HALF : (n + 1) * HALF]
            re, im = piece[:, :WIDTH], piece[:, WIDTH:]
            im, re = im * cos - re * sin, re * cos + im * sin
            top = jnp.where(first, jnp.broadcast_to(ends[n : n + 1], (8, WIDTH)), im[:8])
            sides.append(jnp.concatenate([re, top, im[8:]], 0))
        high, low = split(jnp.concatenate(sides, 1))
        store(pair * 2, dot(back[...], jnp.concatenate([high, high, low], 0)))


def store_pair(ref, first, value):
    for k in range(4):
        n = first + k // 2
        row = ((n % 4) * 5 + n // 4) * 2 + k % 2
        ref[pl.ds(row, ACROSS, stride=40), :] = value[:, k * 128 : (k + 1) * 128]


def grads_kernel(got, across, back, twiddle, table, out, spec, stage_hi, stage_lo, ends, extra):
    load = functools.partial(load_pair, got)
    spectra_of(load, 36, across, twiddle, table, stage_hi, stage_lo, ends, spec)
    for tail in (False, True):

        def take(n):
            rows = spec[36 * HALF + n : 36 * HALF + n + 1] if tail else spec[n * HALF : (n + 1) * HALF]
            return rows[:, :WIDTH], rows[:, WIDTH:]

        def put(n, re, im):
            rows = jnp.concatenate([re, im], 1)
            if tail:
                extra[n : n + 1] = rows
            else:
                high, low = split(rows)
                stage_hi[n * HALF : (n + 1) * HALF] = high
                stage_lo[n * HALF : (n + 1) * HALF] = low

        crosses = []
        for s in range(4):
            own, other = take(16 + s), take(19 - s)
            er, ei = own[0] + other[0], own[1] - other[1]
            re = im = 0.0
            for b in range(4):
                n = b * 4 + s
                (cr, ci), (xr, xi) = take(n), take(20 + n)
                put(n, er * cr + ei * ci, ei * cr - er * ci)
                re = re + (cr * xr + ci * xi)
                im = im + (cr * xi - ci * xr)
            crosses.append((re, im))
        for s in range(4):
            a, b = crosses[s], crosses[3 - s]
            put(16 + s, a[0] + b[0], a[1] - b[1])
    high, low = split(extra[...])
    stage_hi[20 * HALF : 20 * HALF + 32] = high
    stage_lo[20 * HALF : 20 * HALF + 32] = low
    positions_of(
        20, back, twiddle, table, stage_hi, stage_lo, spec, functools.partial(store_pair, out)
    )


def call(kernel, outs, scratch, flops, *args, in_specs=None, out_specs=None, vmem=VMEM, near=False):
    moved = sum(a.size * a.dtype.itemsize for a in args) + sum(4 * math.prod(o) for o in outs)
    options = dict(in_specs=in_specs) if in_specs else {}
    if out_specs:
        options["out_specs"] = out_specs
    return pl.pallas_call(
        kernel,
        out_shape=[(pltpu.VMEM if near else jax.ShapeDtypeStruct)(o, F32) for o in outs],
        scratch_shapes=scratch,
        compiler_params=pltpu.CompilerParams(vmem_limit_bytes=vmem),
        cost_estimate=pl.CostEstimate(flops=flops, bytes_accessed=moved, transcendentals=0),
        **options,
    )(*args)


def exchange(value, units):
    blocks = value.reshape(DEVICES, units, 2, 128)
    return lax.all_to_all(blocks, ("ctx", "ch"), 0, 0, tiled=True).reshape(-1, 128)


def body(inputs, cotangent, filters):
    across, back, twiddle, table = [jnp.asarray(t) for t in tables()]
    far = pl.BlockSpec(memory_space=pltpu.HBM)
    (packed,) = call(
        pack_kernel,
        [(DEVICES * 18, 128)],
        [pltpu.VMEM((9, WIDTH, WIDTH), F32), pltpu.SemaphoreType.DMA((9,))],
        10**9,
        cotangent, filters, inputs,
        in_specs=[far] * 3,
        vmem=PACK_VMEM,
        near=True,
    )
    got = exchange(packed, 9)
    (grads,) = call(
        grads_kernel,
        [(DEVICES * 10, 128)],
        [pltpu.VMEM((36 * HALF + 48, 2 * WIDTH), F32)]
        + [pltpu.VMEM((36 * HALF + 48, 2 * WIDTH), BF)] * 2
        + [pltpu.VMEM((48, WIDTH), F32), pltpu.VMEM((32, 2 * WIDTH), F32)],
        8 * 10**9,
        got, across, back, twiddle, table,
    )
    return tuple(
        call(
            unpack_kernel,
            [(4, WIDTH, WIDTH), (WIDTH, WIDTH)],
            [pltpu.VMEM((5, WIDTH, WIDTH), F32), pltpu.SemaphoreType.DMA((5,))],
            10**9,
            exchange(grads, 5),
            out_specs=[far] * 2,
        )
    )


def solution(mesh):
    in_specs = (P(None, "ctx", "ch"), P(None, "ctx", "ch"), P("ctx", "ch"))
    out_specs = (P(None, "ctx", "ch"), P("ctx", "ch"))
    return jax.shard_map(body, mesh=mesh, in_specs=in_specs, out_specs=out_specs, check_vma=False)
```

time: 132 us -> 129 us (0.977)
  local copies, waits for them, and re-layouts: 3.43 us -> 0.03 us
    unnamed x16 -> x8, local copies, waits for them, and re-layouts: 3.43 us -> 0.03 us
where the time goes in v3:
time: 129 us
  blocking collectives  118 us (91%)
  Pallas kernels  10.5 us (8%)
    all_to_all x2, blocking collectives, exchange(): lax.all_to_all(blocks, ('ctx', 'ch'), 0, 0, tiled=True).reshape(-1, 128)  118 us
    pallas_call x3, Pallas kernels, call(): pl.pallas_call(kernel, out_shape=[(pltpu.VMEM if near else jax.ShapeDtype...  10.5 us

profile of v3, /device:TPU:1, one launch (start us, length us, event | category | flops | bytes accessed | tf_op | source)
XLA Modules:
  0.0 128.8 jit_solution(7769612994392298570)
XLA Ops:
  0.6 4.1 %shard_map.86 = f32[4608,128]{1,0:T(8,128)S(1)} custom-call(f32[4,256,256]{2,1,0:T(8,128)} %cotangent.1, f32[256,256]{1,0:T(8,128)} %filters.1, f32[4,256,256]{2,1,0:T(8,128)} %inputs.1), custom_call_target="tpu_custom_call" | custom-call | flops 1000000000 | bytes 4718592 | tf_op jit(solution)/shard_map/pallas_call | solution.py:214
  4.8 0.0 copy-start
  4.8 0.0 copy-start.1
  4.8 0.0 copy-start.2
  4.8 0.0 copy-start.3
  4.8 73.8 %all_to_all.10 = f32[256,9,2,128]{3,2,1,0:T(2,128)S(1)} all-to-all(f32[256,9,2,128]{3,2,1,0:T(2,128)S(1)} %bitcast.4), channel_id=1, replica_groups=mesh['ctx'=64,'ch'=4] {'ctx','ch'}, dimensions={0} | all-to-all | bytes 4718592 | tf_op jit(solution)/shard_map/all_to_all | solution.py:226
  78.6 0.0 copy-done
  78.6 0.0 copy-done.1
  78.6 0.0 copy-done.2
  78.6 0.0 copy-done.3
  78.7 4.9 %shard_map.87 = f32[2560,128]{1,0:T(8,128)S(1)} custom-call(f32[4608,128]{1,0:T(8,128)S(1)} %bitcast.5, bf16[64,192]{1,0:T(8,128)(2,1)S(1)} %copy-done.3, bf16[64,192]{1,0:T(8,128)(2,1)S(1)} %copy-done.2, f32[4,32,256]{2,1,0:T(8,128)S(1)} %copy-done.1, bf16[1536,512]{1,0:T(8,128)(2,1)S(1)} %copy-done), custom_call_target="tpu_custom_call" | custom-call | flops 8000000000 | bytes 5423104 | tf_op jit(solution)/shard_map/pallas_call | solution.py:214
  83.5 43.8 %all_to_all.11 = f32[256,5,2,128]{3,2,1,0:T(2,128)S(1)} all-to-all(f32[256,5,2,128]{3,2,1,0:T(2,128)S(1)} %bitcast.6), channel_id=1, replica_groups=mesh['ctx'=64,'ch'=4] {'ctx','ch'}, dimensions={0} | all-to-all | bytes 2621440 | tf_op jit(solution)/shard_map/all_to_all | solution.py:226
  127.3 1.5 %shard_map.88 = (f32[4,256,256]{2,1,0:T(8,128)}, f32[256,256]{1,0:T(8,128)}) custom-call(f32[2560,128]{1,0:T(8,128)S(1)} %bitcast.7), custom_call_target="tpu_custom_call" | custom-call | flops 1000000000 | bytes 2621440 | tf_op jit(solution)/shard_map/pallas_call | solution.py:214
Async XLA Ops:
  4.8 73.9 %copy-start = (bf16[1536,512]{1,0:T(8,128)(2,1)S(1)}, bf16[1536,512]{1,0:T(8,128)(2,1)}, u32[]{:S(2)}) copy-start(bf16[1536,512]{1,0:T(8,128)(2,1)} %constant.11.clone.table) | copy-start | bytes 4718596
  4.8 73.9 %copy-start.1 = (f32[4,32,256]{2,1,0:T(8,128)S(1)}, f32[4,32,256]{2,1,0:T(8,128)}, u32[]{:S(2)}) copy-start(f32[4,32,256]{2,1,0:T(8,128)} %constant.10.clone.twiddle) | copy-start | bytes 393220
  4.8 73.8 %copy-start.2 = (bf16[64,192]{1,0:T(8,128)(2,1)S(1)}, bf16[64,192]{1,0:T(8,128)(2,1)}, u32[]{:S(2)}) copy-start(bf16[64,192]{1,0:T(8,128)(2,1)} %constant.9.clone.back) | copy-start | bytes 73732
  4.8 73.8 %copy-start.3 = (bf16[64,192]{1,0:T(8,128)(2,1)S(1)}, bf16[64,192]{1,0:T(8,128)(2,1)}, u32[]{:S(2)}) copy-start(bf16[64,192]{1,0:T(8,128)(2,1)} %constant.8.clone.across) | copy-start | bytes 73732

commit v4 on v3

--- a/solution.py
+++ b/solution.py
@@ -14,6 +14,7 @@
 ACROSS = 64
 DEVICES = 256
 WIDTH = 256
+PART = WIDTH // 2
 PERIOD = ACROSS * WIDTH
 HALF = ACROSS // 2
 FACTOR = 1.0 / (PERIOD * math.sqrt(2.0 * PERIOD))
@@ -49,10 +50,14 @@
     ends = np.zeros((HALF, WIDTH))
     ends[0], ends[1] = c[HALF], s[HALF]
     twiddle = np.stack([c[:HALF], s[:HALF], masked, ends]).astype(np.float32)
-    spin = 2.0 * np.pi * (np.outer(j, j) % WIDTH) / WIDTH
-    c, s = np.cos(spin), np.sin(spin)
-    high, low = two_parts(np.block([[c, -s], [s, c]]))
-    return across, back, twiddle, np.concatenate([high, high, low], 0)
+    j = np.arange(PART)
+    parts = []
+    for turns in (2 * np.outer(j, j), np.outer(j, 2 * j + 1), np.outer(2 * j + 1, j)):
+        spin = 2.0 * np.pi * (turns % WIDTH) / WIDTH
+        c, s = np.cos(spin), np.sin(spin)
+        high, low = two_parts(np.block([[c, -s], [s, c]]))
+        parts.append(np.concatenate([high, high, low], 0))
+    return across, back, twiddle, np.stack(parts)
 
 
 def split(value):
@@ -74,11 +79,13 @@
 def pack_kernel(cotangent, filters, inputs, out, held, sems):
     blocks = [cotangent.at[b] for b in range(4)] + [filters] + [inputs.at[b] for b in range(4)]
     copies = [pltpu.make_async_copy(block, held.at[u], sems.at[u]) for u, block in enumerate(blocks)]
-    for copy in copies:
+    for copy in copies[:3]:
         copy.start()
     place = placement()
     for u, copy in enumerate(copies):
         copy.wait()
+        if u + 3 < len(copies):
+            copies[u + 3].start()
         high, low = split(held[u])
         turned = (dot(high, place) + dot(low, place)).T
         for half in range(2):
@@ -111,8 +118,18 @@
     return jnp.concatenate(pieces, 1)
 
 
-def spin_rows(high, low, table):
-    return dot(jnp.concatenate([high, low, high], 1), table[...])
+def spin_rows(high, low, table, odd):
+    results = []
+    for k, which in enumerate((0, odd)):
+        h = jnp.concatenate([high[:, k * PART : (k + 1) * PART], high[:, (k + 2) * PART : (k + 3) * PART]], 1)
+        l = jnp.concatenate([low[:, k * PART : (k + 1) * PART], low[:, (k + 2) * PART : (k + 3) * PART]], 1)
+        results.append(dot(jnp.concatenate([h, l, h], 1), table[which]))
+    return results
+
+
+def butterfly(value):
+    a, b = value[:, :PART], value[:, PART:]
+    return [a + b, a - b]
 
 
 def spectra_of(load, count, across, twiddle, table, stage_hi, stage_lo, ends, spec):
@@ -125,22 +142,32 @@
             re = part[:HALF, k * WIDTH : (k + 1) * WIDTH]
             im = part[HALF:, k * WIDTH : (k + 1) * WIDTH]
             ends[pair * 2 + k : pair * 2 + k + 1, :] = im[:1]
-            turned.append(jnp.concatenate([re * cos + im * sin, im * masked - re * sin], 1))
+            re, im = re * cos + im * sin, im * masked - re * sin
+            turned.append(jnp.concatenate(butterfly(re) + butterfly(im), 1))
         high, low = split(jnp.concatenate(turned, 0))
         stage_hi[pair * 64 : pair * 64 + 64] = high
         stage_lo[pair * 64 : pair * 64 + 64] = low
     base, more = count * HALF, ends.shape[0]
     last = ends[...]
-    high, low = split(jnp.concatenate([last * twiddle[3, 0:1], -last * twiddle[3, 1:2]], 1))
+    pieces = butterfly(last * twiddle[3, 0:1]) + butterfly(-last * twiddle[3, 1:2])
+    high, low = split(jnp.concatenate(pieces, 1))
     stage_hi[base : base + more] = high
     stage_lo[base : base + more] = low
-    spec[...] = spin_rows(stage_hi[: base + more], stage_lo[: base + more], table)
+    even, odd = spin_rows(stage_hi[: base + more], stage_lo[: base + more], table, 1)
+    spec[:, 0 * PART : 1 * PART] = even[:, :PART]
+    spec[:, 1 * PART : 2 * PART] = odd[:, :PART]
+    spec[:, 2 * PART : 3 * PART] = even[:, PART:]
+    spec[:, 3 * PART : 4 * PART] = odd[:, PART:]
 
 
 def positions_of(count, back, twiddle, table, stage_hi, stage_lo, spec, store):
     base = count * HALF
     size = base + 32
-    spec[:size] = spin_rows(stage_hi[:size], stage_lo[:size], table)
+    even, odd = spin_rows(stage_hi[:size], stage_lo[:size], table, 2)
+    spec[:size, 0 * PART : 1 * PART] = even[:, :PART] + odd[:, :PART]
+    spec[:size, 1 * PART : 2 * PART] = even[:, :PART] - odd[:, :PART]
+    spec[:size, 2 * PART : 3 * PART] = even[:, PART:] + odd[:, PART:]
+    spec[:size, 3 * PART : 4 * PART] = even[:, PART:] - odd[:, PART:]
     cos, sin = twiddle[0], twiddle[1]
     first = lax.broadcasted_iota(jnp.int32, (8, WIDTH), 0) == 0
     ends = spec[base:size]

time: 129 us -> 128 us (level)
  Pallas kernels: 10.5 us -> 9.07 us
    pallas_call x3, Pallas kernels: 10.5 us -> 9.07 us  [call(): pl.pallas_call(kernel, out_shape=[(pltpu.VMEM if near else jax.ShapeDtype...]
where the time goes in v4:
time: 128 us; the launch traced here: 127 us
  blocking collectives  118 us (92%)
  Pallas kernels  9.07 us (7%)
    all_to_all x2, blocking collectives, exchange(): lax.all_to_all(blocks, ('ctx', 'ch'), 0, 0, tiled=True).reshape(-1, 128)  118 us
    pallas_call x3, Pallas kernels, call(): pl.pallas_call(kernel, out_shape=[(pltpu.VMEM if near else jax.ShapeDtype...  9.07 us

profile of v4, /device:TPU:1, one launch (start us, length us, event | category | flops | bytes accessed | tf_op | source)
XLA Modules:
  0.0 127.4 jit_solution(3465018172327575085)
XLA Ops:
  0.6 4.1 %shard_map.86 = f32[4608,128]{1,0:T(8,128)S(1)} custom-call(f32[4,256,256]{2,1,0:T(8,128)} %cotangent.1, f32[256,256]{1,0:T(8,128)} %filters.1, f32[4,256,256]{2,1,0:T(8,128)} %inputs.1), custom_call_target="tpu_custom_call" | custom-call | flops 1000000000 | bytes 4718592 | tf_op jit(solution)/shard_map/pallas_call | solution.py:241
  4.8 0.0 copy-start
  4.8 0.0 copy-start.1
  4.8 0.0 copy-start.2
  4.8 0.0 copy-start.3
  4.8 73.8 %all_to_all.10 = f32[256,9,2,128]{3,2,1,0:T(2,128)S(1)} all-to-all(f32[256,9,2,128]{3,2,1,0:T(2,128)S(1)} %bitcast.4), channel_id=1, replica_groups=mesh['ctx'=64,'ch'=4] {'ctx','ch'}, dimensions={0} | all-to-all | bytes 4718592 | tf_op jit(solution)/shard_map/all_to_all | solution.py:253
  78.6 0.0 copy-done
  78.6 0.0 copy-done.1
  78.6 0.0 copy-done.2
  78.6 0.0 copy-done.3
  78.7 3.5 %shard_map.87 = f32[2560,128]{1,0:T(8,128)S(1)} custom-call(f32[4608,128]{1,0:T(8,128)S(1)} %bitcast.5, bf16[64,192]{1,0:T(8,128)(2,1)S(1)} %copy-done.3, bf16[64,192]{1,0:T(8,128)(2,1)S(1)} %copy-done.2, f32[4,32,256]{2,1,0:T(8,128)S(1)} %copy-done.1, bf16[3,768,256]{2,1,0:T(8,128)(2,1)S(1)} %copy-done), custom_call_target="tpu_custom_call" | custom-call | flops 8000000000 | bytes 5029888 | tf_op jit(solution)/shard_map/pallas_call | solution.py:241
  82.1 43.8 %all_to_all.11 = f32[256,5,2,128]{3,2,1,0:T(2,128)S(1)} all-to-all(f32[256,5,2,128]{3,2,1,0:T(2,128)S(1)} %bitcast.6), channel_id=1, replica_groups=mesh['ctx'=64,'ch'=4] {'ctx','ch'}, dimensions={0} | all-to-all | bytes 2621440 | tf_op jit(solution)/shard_map/all_to_all | solution.py:253
  125.9 1.5 %shard_map.88 = (f32[4,256,256]{2,1,0:T(8,128)}, f32[256,256]{1,0:T(8,128)}) custom-call(f32[2560,128]{1,0:T(8,128)S(1)} %bitcast.7), custom_call_target="tpu_custom_call" | custom-call | flops 1000000000 | bytes 2621440 | tf_op jit(solution)/shard_map/pallas_call | solution.py:241
Async XLA Ops:
  4.8 73.9 %copy-start = (bf16[3,768,256]{2,1,0:T(8,128)(2,1)S(1)}, bf16[3,768,256]{2,1,0:T(8,128)(2,1)}, u32[]{:S(2)}) copy-start(bf16[3,768,256]{2,1,0:T(8,128)(2,1)} %constant.11.clone.table) | copy-start | bytes 3538948
  4.8 73.9 %copy-start.1 = (f32[4,32,256]{2,1,0:T(8,128)S(1)}, f32[4,32,256]{2,1,0:T(8,128)}, u32[]{:S(2)}) copy-start(f32[4,32,256]{2,1,0:T(8,128)} %constant.10.clone.twiddle) | copy-start | bytes 393220
  4.8 73.8 %copy-start.2 = (bf16[64,192]{1,0:T(8,128)(2,1)S(1)}, bf16[64,192]{1,0:T(8,128)(2,1)}, u32[]{:S(2)}) copy-start(bf16[64,192]{1,0:T(8,128)(2,1)} %constant.9.clone.back) | copy-start | bytes 73732
  4.8 73.8 %copy-start.3 = (bf16[64,192]{1,0:T(8,128)(2,1)S(1)}, bf16[64,192]{1,0:T(8,128)(2,1)}, u32[]{:S(2)}) copy-start(bf16[64,192]{1,0:T(8,128)(2,1)} %constant.8.clone.across) | copy-start | bytes 73732

commit v5 on v4

--- a/solution.py
+++ b/solution.py
@@ -18,6 +18,7 @@
 PERIOD = ACROSS * WIDTH
 HALF = ACROSS // 2
 FACTOR = 1.0 / (PERIOD * math.sqrt(2.0 * PERIOD))
+AHEAD = 7
 VMEM = 48 * 1024 * 1024
 PACK_VMEM = 56 * 1024 * 1024
 
@@ -69,44 +70,57 @@
     return jnp.dot(left, right, preferred_element_type=F32)
 
 
-def placement():
+def mirrored(value):
+    back = 7 - lax.broadcasted_iota(jnp.int32, (8, 128), 0)
+    columns = []
+    for half in range(2):
+        lanes = slice(half * 128, (half + 1) * 128)
+        groups = [value[k * 8 : (k + 1) * 8, lanes] for k in reversed(range(value.shape[0] // 8))]
+        columns.append(
+            jnp.concatenate([jnp.take_along_axis(group, back, axis=0) for group in groups], 0)
+        )
+    return jnp.concatenate(columns, 1)
+
+
+def both_halves(run):
     upper = lax.axis_index("ch") >= 2
-    row = lax.broadcasted_iota(jnp.int32, (WIDTH, WIDTH), 0)
-    column = lax.broadcasted_iota(jnp.int32, (WIDTH, WIDTH), 1)
-    return jnp.where(column == jnp.where(upper, WIDTH - 1 - row, row), 1.0, 0.0).astype(BF)
+    pl.when(upper)(functools.partial(run, mirrored))
+    pl.when(jnp.logical_not(upper))(functools.partial(run, lambda value: value))
 
 
 def pack_kernel(cotangent, filters, inputs, out, held, sems):
     blocks = [cotangent.at[b] for b in range(4)] + [filters] + [inputs.at[b] for b in range(4)]
     copies = [pltpu.make_async_copy(block, held.at[u], sems.at[u]) for u, block in enumerate(blocks)]
-    for copy in copies[:3]:
+    for copy in copies[:AHEAD]:
         copy.start()
-    place = placement()
-    for u, copy in enumerate(copies):
-        copy.wait()
-        if u + 3 < len(copies):
-            copies[u + 3].start()
-        high, low = split(held[u])
-        turned = (dot(high, place) + dot(low, place)).T
-        for half in range(2):
-            out[pl.ds(u * 2 + half, DEVICES, stride=18), :] = turned[:, half * 128 : (half + 1) * 128]
+
+    def run(order):
+        for u, copy in enumerate(copies):
+            copy.wait()
+            if u + AHEAD < len(copies):
+                copies[u + AHEAD].start()
+            turned = order(held[u].T)
+            for half in range(2):
+                out[pl.ds(u * 2 + half, DEVICES, stride=18), :] = turned[
+                    :, half * 128 : (half + 1) * 128
+                ]
+
+    both_halves(run)
 
 
 def unpack_kernel(ref, inputs, filters, held, sems):
-    place = placement()
     blocks = [inputs.at[b] for b in range(4)] + [filters]
-    copies = []
-    for u, block in enumerate(blocks):
-        halves = [ref[pl.ds(u * 2 + half, DEVICES, stride=10), :] for half in range(2)]
-        value = jnp.concatenate(halves, 1).T
-        total = jnp.zeros((WIDTH, WIDTH), F32)
-        for part in split(value):
-            total = total + dot(part, place)
-        held[u] = total
-        copies.append(pltpu.make_async_copy(held.at[u], block, sems.at[u]))
-        copies[-1].start()
-    for copy in copies:
-        copy.wait()
+    copies = [pltpu.make_async_copy(held.at[u], block, sems.at[u]) for u, block in enumerate(blocks)]
+
+    def run(order):
+        for u, copy in enumerate(copies):
+            halves = [ref[pl.ds(u * 2 + half, DEVICES, stride=10), :] for half in range(2)]
+            held[u] = order(jnp.concatenate(halves, 1)).T
+            copy.start()
+        for copy in copies:
+            copy.wait()
+
+    both_halves(run)
 
 
 def load_pair(ref, first):

time: 128 us -> 126 us (0.984)
  Pallas kernels: 9.07 us -> 7.06 us
    pallas_call x3, Pallas kernels: 9.07 us -> 7.06 us  [call(): pl.pallas_call(kernel, out_shape=[(pltpu.VMEM if near else jax.ShapeDtype...]
where the time goes in v5:
time: 126 us; the launch traced here: 125 us
  blocking collectives  118 us (94%)
  Pallas kernels  7.06 us (6%)
    all_to_all x2, blocking collectives, exchange(): lax.all_to_all(blocks, ('ctx', 'ch'), 0, 0, tiled=True).reshape(-1, 128)  118 us
    pallas_call x3, Pallas kernels, call(): pl.pallas_call(kernel, out_shape=[(pltpu.VMEM if near else jax.ShapeDtype...  7.06 us

profile of v5, /device:TPU:1, one launch (start us, length us, event | category | flops | bytes accessed | tf_op | source)
XLA Modules:
  0.0 125.4 jit_solution(11288694983604064017)
XLA Ops:
  0.6 2.4 %shard_map.86 = f32[4608,128]{1,0:T(8,128)S(1)} custom-call(f32[4,256,256]{2,1,0:T(8,128)} %cotangent.1, f32[256,256]{1,0:T(8,128)} %filters.1, f32[4,256,256]{2,1,0:T(8,128)} %inputs.1), custom_call_target="tpu_custom_call" | custom-call | flops 1000000000 | bytes 4718592 | tf_op jit(solution)/shard_map/pallas_call | solution.py:255
  3.0 0.0 copy-start
  3.0 0.0 copy-start.1
  3.0 0.0 copy-start.2
  3.0 0.0 copy-start.3
  3.1 73.8 %all_to_all.10 = f32[256,9,2,128]{3,2,1,0:T(2,128)S(1)} all-to-all(f32[256,9,2,128]{3,2,1,0:T(2,128)S(1)} %bitcast.4), channel_id=1, replica_groups=mesh['ctx'=64,'ch'=4] {'ctx','ch'}, dimensions={0} | all-to-all | bytes 4718592 | tf_op jit(solution)/shard_map/all_to_all | solution.py:267
  76.9 0.0 copy-done
  76.9 0.0 copy-done.1
  76.9 0.0 copy-done.2
  76.9 0.0 copy-done.3
  76.9 3.5 %shard_map.87 = f32[2560,128]{1,0:T(8,128)S(1)} custom-call(f32[4608,128]{1,0:T(8,128)S(1)} %bitcast.5, bf16[64,192]{1,0:T(8,128)(2,1)S(1)} %copy-done.3, bf16[64,192]{1,0:T(8,128)(2,1)S(1)} %copy-done.2, f32[4,32,256]{2,1,0:T(8,128)S(1)} %copy-done.1, bf16[3,768,256]{2,1,0:T(8,128)(2,1)S(1)} %copy-done), custom_call_target="tpu_custom_call" | custom-call | flops 8000000000 | bytes 5029888 | tf_op jit(solution)/shard_map/pallas_call | solution.py:255
  80.4 43.8 %all_to_all.11 = f32[256,5,2,128]{3,2,1,0:T(2,128)S(1)} all-to-all(f32[256,5,2,128]{3,2,1,0:T(2,128)S(1)} %bitcast.6), channel_id=1, replica_groups=mesh['ctx'=64,'ch'=4] {'ctx','ch'}, dimensions={0} | all-to-all | bytes 2621440 | tf_op jit(solution)/shard_map/all_to_all | solution.py:267
  124.2 1.2 shard_map.88
Async XLA Ops:
  3.0 73.9 %copy-start = (bf16[3,768,256]{2,1,0:T(8,128)(2,1)S(1)}, bf16[3,768,256]{2,1,0:T(8,128)(2,1)}, u32[]{:S(2)}) copy-start(bf16[3,768,256]{2,1,0:T(8,128)(2,1)} %constant.11.clone.table) | copy-start | bytes 3538948
  3.0 73.9 %copy-start.1 = (f32[4,32,256]{2,1,0:T(8,128)S(1)}, f32[4,32,256]{2,1,0:T(8,128)}, u32[]{:S(2)}) copy-start(f32[4,32,256]{2,1,0:T(8,128)} %constant.10.clone.twiddle) | copy-start | bytes 393220
  3.0 73.8 %copy-start.2 = (bf16[64,192]{1,0:T(8,128)(2,1)S(1)}, bf16[64,192]{1,0:T(8,128)(2,1)}, u32[]{:S(2)}) copy-start(bf16[64,192]{1,0:T(8,128)(2,1)} %constant.9.clone.back) | copy-start | bytes 73732
  3.0 73.8 %copy-start.3 = (bf16[64,192]{1,0:T(8,128)(2,1)S(1)}, bf16[64,192]{1,0:T(8,128)(2,1)}, u32[]{:S(2)}) copy-start(bf16[64,192]{1,0:T(8,128)(2,1)} %constant.8.clone.across) | copy-start | bytes 73732

commit v6 on v5

--- a/solution.py
+++ b/solution.py
@@ -141,6 +141,11 @@
     return results
 
 
+def shares(size, parts):
+    step = size // parts
+    return [slice(at, at + step) for at in range(0, size, step)]
+
+
 def butterfly(value):
     a, b = value[:, :PART], value[:, PART:]
     return [a + b, a - b]
@@ -167,21 +172,23 @@
     high, low = split(jnp.concatenate(pieces, 1))
     stage_hi[base : base + more] = high
     stage_lo[base : base + more] = low
-    even, odd = spin_rows(stage_hi[: base + more], stage_lo[: base + more], table, 1)
-    spec[:, 0 * PART : 1 * PART] = even[:, :PART]
-    spec[:, 1 * PART : 2 * PART] = odd[:, :PART]
-    spec[:, 2 * PART : 3 * PART] = even[:, PART:]
-    spec[:, 3 * PART : 4 * PART] = odd[:, PART:]
+    for rows in shares(base + more, 3):
+        even, odd = spin_rows(stage_hi[rows], stage_lo[rows], table, 1)
+        spec[rows, 0 * PART : 1 * PART] = even[:, :PART]
+        spec[rows, 1 * PART : 2 * PART] = odd[:, :PART]
+        spec[rows, 2 * PART : 3 * PART] = even[:, PART:]
+        spec[rows, 3 * PART : 4 * PART] = odd[:, PART:]
 
 
 def positions_of(count, back, twiddle, table, stage_hi, stage_lo, spec, store):
     base = count * HALF
     size = base + 32
-    even, odd = spin_rows(stage_hi[:size], stage_lo[:size], table, 2)
-    spec[:size, 0 * PART : 1 * PART] = even[:, :PART] + odd[:, :PART]
-    spec[:size, 1 * PART : 2 * PART] = even[:, :PART] - odd[:, :PART]
-    spec[:size, 2 * PART : 3 * PART] = even[:, PART:] + odd[:, PART:]
-    spec[:size, 3 * PART : 4 * PART] = even[:, PART:] - odd[:, PART:]
+    for rows in shares(size, 2):
+        even, odd = spin_rows(stage_hi[rows], stage_lo[rows], table, 2)
+        spec[rows, 0 * PART : 1 * PART] = even[:, :PART] + odd[:, :PART]
+        spec[rows, 1 * PART : 2 * PART] = even[:, :PART] - odd[:, :PART]
+        spec[rows, 2 * PART : 3 * PART] = even[:, PART:] + odd[:, PART:]
+        spec[rows, 3 * PART : 4 * PART] = even[:, PART:] - odd[:, PART:]
     cos, sin = twiddle[0], twiddle[1]
     first = lax.broadcasted_iota(jnp.int32, (8, WIDTH), 0) == 0
     ends = spec[base:size]

time: 126 us -> 125 us (level)
  no operation moved by 1% of the time
where the time goes in v6:
time: 125 us
  blocking collectives  118 us (94%)
  Pallas kernels  6.93 us (6%)
    all_to_all x2, blocking collectives, exchange(): lax.all_to_all(blocks, ('ctx', 'ch'), 0, 0, tiled=True).reshape(-1, 128)  118 us
    pallas_call x3, Pallas kernels, call(): pl.pallas_call(kernel, out_shape=[(pltpu.VMEM if near else jax.ShapeDtype...  6.93 us

profile of v6, /device:TPU:1, one launch (start us, length us, event | category | flops | bytes accessed | tf_op | source)
XLA Modules:
  0.0 125.3 jit_solution(13399316964374186377)
XLA Ops:
  0.6 2.4 %shard_map.86 = f32[4608,128]{1,0:T(8,128)S(1)} custom-call(f32[4,256,256]{2,1,0:T(8,128)} %cotangent.1, f32[256,256]{1,0:T(8,128)} %filters.1, f32[4,256,256]{2,1,0:T(8,128)} %inputs.1), custom_call_target="tpu_custom_call" | custom-call | flops 1000000000 | bytes 4718592 | tf_op jit(solution)/shard_map/pallas_call | solution.py:262
  3.0 0.0 copy-start
  3.0 0.0 copy-start.1
  3.0 0.0 copy-start.2
  3.0 0.0 copy-start.3
  3.1 73.8 %all_to_all.10 = f32[256,9,2,128]{3,2,1,0:T(2,128)S(1)} all-to-all(f32[256,9,2,128]{3,2,1,0:T(2,128)S(1)} %bitcast.4), channel_id=1, replica_groups=mesh['ctx'=64,'ch'=4] {'ctx','ch'}, dimensions={0} | all-to-all | bytes 4718592 | tf_op jit(solution)/shard_map/all_to_all | solution.py:274
  76.9 0.0 copy-done
  76.9 0.0 copy-done.1
  76.9 0.0 copy-done.2
  76.9 0.0 copy-done.3
  76.9 3.3 %shard_map.87 = f32[2560,128]{1,0:T(8,128)S(1)} custom-call(f32[4608,128]{1,0:T(8,128)S(1)} %bitcast.5, bf16[64,192]{1,0:T(8,128)(2,1)S(1)} %copy-done.3, bf16[64,192]{1,0:T(8,128)(2,1)S(1)} %copy-done.2, f32[4,32,256]{2,1,0:T(8,128)S(1)} %copy-done.1, bf16[3,768,256]{2,1,0:T(8,128)(2,1)S(1)} %copy-done), custom_call_target="tpu_custom_call" | custom-call | flops 8000000000 | bytes 5029888 | tf_op jit(solution)/shard_map/pallas_call | solution.py:262
  80.2 43.8 %all_to_all.11 = f32[256,5,2,128]{3,2,1,0:T(2,128)S(1)} all-to-all(f32[256,5,2,128]{3,2,1,0:T(2,128)S(1)} %bitcast.6), channel_id=1, replica_groups=mesh['ctx'=64,'ch'=4] {'ctx','ch'}, dimensions={0} | all-to-all | bytes 2621440 | tf_op jit(solution)/shard_map/all_to_all | solution.py:274
  124.0 1.2 shard_map.88
Async XLA Ops:
  3.0 73.9 %copy-start = (bf16[3,768,256]{2,1,0:T(8,128)(2,1)S(1)}, bf16[3,768,256]{2,1,0:T(8,128)(2,1)}, u32[]{:S(2)}) copy-start(bf16[3,768,256]{2,1,0:T(8,128)(2,1)} %constant.11.clone.table) | copy-start | bytes 3538948
  3.0 73.9 %copy-start.1 = (f32[4,32,256]{2,1,0:T(8,128)S(1)}, f32[4,32,256]{2,1,0:T(8,128)}, u32[]{:S(2)}) copy-start(f32[4,32,256]{2,1,0:T(8,128)} %constant.10.clone.twiddle) | copy-start | bytes 393220
  3.0 73.8 %copy-start.2 = (bf16[64,192]{1,0:T(8,128)(2,1)S(1)}, bf16[64,192]{1,0:T(8,128)(2,1)}, u32[]{:S(2)}) copy-start(bf16[64,192]{1,0:T(8,128)(2,1)} %constant.9.clone.back) | copy-start | bytes 73732
  3.0 73.8 %copy-start.3 = (bf16[64,192]{1,0:T(8,128)(2,1)S(1)}, bf16[64,192]{1,0:T(8,128)(2,1)}, u32[]{:S(2)}) copy-start(bf16[64,192]{1,0:T(8,128)(2,1)} %constant.8.clone.across) | copy-start | bytes 73732

commit v7 on v6

--- a/solution.py
+++ b/solution.py
@@ -12,7 +12,7 @@
 BF = jnp.bfloat16
 F32 = jnp.float32
 ACROSS = 64
-DEVICES = 256
+GROUP = 2 * ACROSS
 WIDTH = 256
 PART = WIDTH // 2
 PERIOD = ACROSS * WIDTH
@@ -100,9 +100,9 @@
             if u + AHEAD < len(copies):
                 copies[u + AHEAD].start()
             turned = order(held[u].T)
-            for half in range(2):
-                out[pl.ds(u * 2 + half, DEVICES, stride=18), :] = turned[
-                    :, half * 128 : (half + 1) * 128
+            for k in range(4):
+                out[pl.ds(u * 4 + k, GROUP, stride=36), :] = turned[
+                    k // 2 * GROUP : (k // 2 + 1) * GROUP, k % 2 * 128 : (k % 2 + 1) * 128
                 ]
 
     both_halves(run)
@@ -114,21 +114,26 @@
 
     def run(order):
         for u, copy in enumerate(copies):
-            halves = [ref[pl.ds(u * 2 + half, DEVICES, stride=10), :] for half in range(2)]
-            held[u] = order(jnp.concatenate(halves, 1)).T
+            parts = [ref[pl.ds(u * 4 + k, GROUP, stride=20), :] for k in range(4)]
+            sides = [jnp.concatenate(parts[k : k + 2], 1) for k in (0, 2)]
+            held[u] = order(jnp.concatenate(sides, 0)).T
             copy.start()
         for copy in copies:
             copy.wait()
 
     both_halves(run)
+
+
+def row_of(n, half, units):
+    side, slot = ((0, 0), (0, 1), (1, 1), (1, 0))[n % 4]
+    return ((side * units + n // 4) * 2 + slot) * 2 + half
 
 
 def load_pair(ref, first):
     pieces = []
     for n in (first, first + 1):
         for half in range(2):
-            row = ((n % 4) * 9 + n // 4) * 2 + half
-            pieces.append(ref[pl.ds(row, ACROSS, stride=72), :])
+            pieces.append(ref[pl.ds(row_of(n, half, 9), ACROSS, stride=72), :])
     return jnp.concatenate(pieces, 1)
 
 
@@ -209,8 +214,7 @@
 def store_pair(ref, first, value):
     for k in range(4):
         n = first + k // 2
-        row = ((n % 4) * 5 + n // 4) * 2 + k % 2
-        ref[pl.ds(row, ACROSS, stride=40), :] = value[:, k * 128 : (k + 1) * 128]
+        ref[pl.ds(row_of(n, k % 2, 5), ACROSS, stride=40), :] = value[:, k * 128 : (k + 1) * 128]
 
 
 def grads_kernel(got, across, back, twiddle, table, out, spec, stage_hi, stage_lo, ends, extra):
@@ -270,8 +274,11 @@
 
 
 def exchange(value, units):
-    blocks = value.reshape(DEVICES, units, 2, 128)
-    return lax.all_to_all(blocks, ("ctx", "ch"), 0, 0, tiled=True).reshape(-1, 128)
+    groups = [[i * 4 + s for i in range(ACROSS) for s in (low, 3 - low)] for low in range(2)]
+    blocks = value.reshape(GROUP, units, 4, 128)
+    return lax.all_to_all(
+        blocks, ("ctx", "ch"), 0, 0, axis_index_groups=groups, tiled=True
+    ).reshape(-1, 128)
 
 
 def body(inputs, cotangent, filters):
@@ -279,7 +286,7 @@
     far = pl.BlockSpec(memory_space=pltpu.HBM)
     (packed,) = call(
         pack_kernel,
-        [(DEVICES * 18, 128)],
+        [(GROUP * 36, 128)],
         [pltpu.VMEM((9, WIDTH, WIDTH), F32), pltpu.SemaphoreType.DMA((9,))],
         10**9,
         cotangent, filters, inputs,
@@ -290,7 +297,7 @@
     got = exchange(packed, 9)
     (grads,) = call(
         grads_kernel,
-        [(DEVICES * 10, 128)],
+        [(GROUP * 20, 128)],
         [pltpu.VMEM((36 * HALF + 48, 2 * WIDTH), F32)]
         + [pltpu.VMEM((36 * HALF + 48, 2 * WIDTH), BF)] * 2
         + [pltpu.VMEM((48, WIDTH), F32), pltpu.VMEM((32, 2 * WIDTH), F32)],

time: 125 us -> 125 us (level); the launches traced: 125 us -> 124 us
  blocking collectives: 118 us -> 116 us
    all_to_all x2, blocking collectives: 118 us -> 116 us  [exchange(): lax.all_to_all(blocks, ('ctx', 'ch'), 0, 0, axis_index_groups=groups, til...]
where the time goes in v7:
time: 125 us; the launch traced here: 124 us
  blocking collectives  116 us (93%)
  Pallas kernels  6.93 us (6%)
    all_to_all x2, blocking collectives, exchange(): lax.all_to_all(blocks, ('ctx', 'ch'), 0, 0, axis_index_groups=groups, til...  116 us
    pallas_call x3, Pallas kernels, call(): pl.pallas_call(kernel, out_shape=[(pltpu.VMEM if near else jax.ShapeDtype...  6.93 us

profile of v7, /device:TPU:1, one launch (start us, length us, event | category | flops | bytes accessed | tf_op | source)
XLA Modules:
  0.0 123.7 jit_solution(15353282389660058403)
XLA Ops:
  0.6 2.4 %shard_map.86 = f32[4608,128]{1,0:T(8,128)S(1)} custom-call(f32[4,256,256]{2,1,0:T(8,128)} %cotangent.1, f32[256,256]{1,0:T(8,128)} %filters.1, f32[4,256,256]{2,1,0:T(8,128)} %inputs.1), custom_call_target="tpu_custom_call" | custom-call | flops 1000000000 | bytes 4718592 | tf_op jit(solution)/shard_map/pallas_call | solution.py:266
  3.0 0.0 copy-start
  3.0 0.0 copy-start.1
  3.0 0.0 copy-start.2
  3.0 0.0 copy-start.3
  3.1 72.5 %all_to_all.10 = f32[128,9,4,128]{3,2,1,0:T(4,128)S(1)} all-to-all(f32[128,9,4,128]{3,2,1,0:T(4,128)S(1)} %bitcast.4), channel_id=1, replica_groups={{0,3,4,7,8,11,12,15,16,19,20,23,24,27,28,31,32,35,36,39,40,43,44,47,48,..., dimensions={0} | all-to-all | bytes 4718592 | tf_op jit(solution)/shard_map/all_to_all | solution.py:279
  75.6 0.0 copy-done
  75.6 0.0 copy-done.1
  75.6 0.0 copy-done.2
  75.6 0.0 copy-done.3
  75.6 3.3 %shard_map.87 = f32[2560,128]{1,0:T(8,128)S(1)} custom-call(f32[4608,128]{1,0:T(8,128)S(1)} %bitcast.5, bf16[64,192]{1,0:T(8,128)(2,1)S(1)} %copy-done.3, bf16[64,192]{1,0:T(8,128)(2,1)S(1)} %copy-done.2, f32[4,32,256]{2,1,0:T(8,128)S(1)} %copy-done.1, bf16[3,768,256]{2,1,0:T(8,128)(2,1)S(1)} %copy-done), custom_call_target="tpu_custom_call" | custom-call | flops 8000000000 | bytes 5029888 | tf_op jit(solution)/shard_map/pallas_call | solution.py:266
  78.9 43.5 %all_to_all.11 = f32[128,5,4,128]{3,2,1,0:T(4,128)S(1)} all-to-all(f32[128,5,4,128]{3,2,1,0:T(4,128)S(1)} %bitcast.6), channel_id=1, replica_groups={{0,3,4,7,8,11,12,15,16,19,20,23,24,27,28,31,32,35,36,39,40,43,44,47,48,..., dimensions={0} | all-to-all | bytes 2621440 | tf_op jit(solution)/shard_map/all_to_all | solution.py:279
  122.4 1.2 shard_map.88
Async XLA Ops:
  3.0 72.6 %copy-start = (bf16[3,768,256]{2,1,0:T(8,128)(2,1)S(1)}, bf16[3,768,256]{2,1,0:T(8,128)(2,1)}, u32[]{:S(2)}) copy-start(bf16[3,768,256]{2,1,0:T(8,128)(2,1)} %constant.11.clone.table) | copy-start | bytes 3538948
  3.0 72.6 %copy-start.1 = (f32[4,32,256]{2,1,0:T(8,128)S(1)}, f32[4,32,256]{2,1,0:T(8,128)}, u32[]{:S(2)}) copy-start(f32[4,32,256]{2,1,0:T(8,128)} %constant.10.clone.twiddle) | copy-start | bytes 393220
  3.0 72.5 %copy-start.2 = (bf16[64,192]{1,0:T(8,128)(2,1)S(1)}, bf16[64,192]{1,0:T(8,128)(2,1)}, u32[]{:S(2)}) copy-start(bf16[64,192]{1,0:T(8,128)(2,1)} %constant.9.clone.back) | copy-start | bytes 73732
  3.0 72.5 %copy-start.3 = (bf16[64,192]{1,0:T(8,128)(2,1)S(1)}, bf16[64,192]{1,0:T(8,128)(2,1)}, u32[]{:S(2)}) copy-start(bf16[64,192]{1,0:T(8,128)(2,1)} %constant.8.clone.across) | copy-start | bytes 73732

commit v8 on v7

--- a/solution.py
+++ b/solution.py
@@ -18,7 +18,7 @@
 PERIOD = ACROSS * WIDTH
 HALF = ACROSS // 2
 FACTOR = 1.0 / (PERIOD * math.sqrt(2.0 * PERIOD))
-AHEAD = 7
+AHEAD = 14
 VMEM = 48 * 1024 * 1024
 PACK_VMEM = 56 * 1024 * 1024
 
@@ -72,14 +72,8 @@
 
 def mirrored(value):
     back = 7 - lax.broadcasted_iota(jnp.int32, (8, 128), 0)
-    columns = []
-    for half in range(2):
-        lanes = slice(half * 128, (half + 1) * 128)
-        groups = [value[k * 8 : (k + 1) * 8, lanes] for k in reversed(range(value.shape[0] // 8))]
-        columns.append(
-            jnp.concatenate([jnp.take_along_axis(group, back, axis=0) for group in groups], 0)
-        )
-    return jnp.concatenate(columns, 1)
+    groups = [value[k * 8 : (k + 1) * 8] for k in reversed(range(value.shape[0] // 8))]
+    return jnp.concatenate([jnp.take_along_axis(group, back, axis=0) for group in groups], 0)
 
 
 def both_halves(run):
@@ -88,35 +82,39 @@
     pl.when(jnp.logical_not(upper))(functools.partial(run, lambda value: value))
 
 
+def half_blocks(stacked, single, count):
+    whole = [stacked.at[b] for b in range(count)] + ([single] if single is not None else [])
+    return [block.at[pl.ds(half * PART, PART)] for block in whole for half in range(2)]
+
+
 def pack_kernel(cotangent, filters, inputs, out, held, sems):
-    blocks = [cotangent.at[b] for b in range(4)] + [filters] + [inputs.at[b] for b in range(4)]
-    copies = [pltpu.make_async_copy(block, held.at[u], sems.at[u]) for u, block in enumerate(blocks)]
+    blocks = half_blocks(cotangent, filters, 4) + half_blocks(inputs, None, 4)
+    copies = [pltpu.make_async_copy(block, held.at[h], sems.at[h]) for h, block in enumerate(blocks)]
     for copy in copies[:AHEAD]:
         copy.start()
 
     def run(order):
-        for u, copy in enumerate(copies):
+        for h, copy in enumerate(copies):
             copy.wait()
-            if u + AHEAD < len(copies):
-                copies[u + AHEAD].start()
-            turned = order(held[u].T)
-            for k in range(4):
-                out[pl.ds(u * 4 + k, GROUP, stride=36), :] = turned[
-                    k // 2 * GROUP : (k // 2 + 1) * GROUP, k % 2 * 128 : (k % 2 + 1) * 128
-                ]
+            if h + AHEAD < len(copies):
+                copies[h + AHEAD].start()
+            turned = order(held[h].T)
+            for slot in range(2):
+                row = (h // 2) * 4 + slot * 2 + h % 2
+                out[pl.ds(row, GROUP, stride=36), :] = turned[slot * GROUP : (slot + 1) * GROUP]
 
     both_halves(run)
 
 
 def unpack_kernel(ref, inputs, filters, held, sems):
-    blocks = [inputs.at[b] for b in range(4)] + [filters]
-    copies = [pltpu.make_async_copy(held.at[u], block, sems.at[u]) for u, block in enumerate(blocks)]
+    blocks = half_blocks(inputs, filters, 4)
+    copies = [pltpu.make_async_copy(held.at[h], block, sems.at[h]) for h, block in enumerate(blocks)]
 
     def run(order):
-        for u, copy in enumerate(copies):
-            parts = [ref[pl.ds(u * 4 + k, GROUP, stride=20), :] for k in range(4)]
-            sides = [jnp.concatenate(parts[k : k + 2], 1) for k in (0, 2)]
-            held[u] = order(jnp.concatenate(sides, 0)).T
+        for h, copy in enumerate(copies):
+            rows = [(h // 2) * 4 + slot * 2 + h % 2 for slot in range(2)]
+            parts = [ref[pl.ds(row, GROUP, stride=20), :] for row in rows]
+            held[h] = order(jnp.concatenate(parts, 0)).T
             copy.start()
         for copy in copies:
             copy.wait()
@@ -287,7 +285,7 @@
     (packed,) = call(
         pack_kernel,
         [(GROUP * 36, 128)],
-        [pltpu.VMEM((9, WIDTH, WIDTH), F32), pltpu.SemaphoreType.DMA((9,))],
+        [pltpu.VMEM((18, PART, WIDTH), F32), pltpu.SemaphoreType.DMA((18,))],
         10**9,
         cotangent, filters, inputs,
         in_specs=[far] * 3,
@@ -308,7 +306,7 @@
         call(
             unpack_kernel,
             [(4, WIDTH, WIDTH), (WIDTH, WIDTH)],
-            [pltpu.VMEM((5, WIDTH, WIDTH), F32), pltpu.SemaphoreType.DMA((5,))],
+            [pltpu.VMEM((10, PART, WIDTH), F32), pltpu.SemaphoreType.DMA((10,))],
             10**9,
             exchange(grads, 5),
             out_specs=[far] * 2,

time: 125 us -> 125 us (level)
  no operation moved by 1% of the time
where the time goes in v8:
time: 125 us; the launch traced here: 124 us
  blocking collectives  116 us (93%)
  Pallas kernels  7.45 us (6%)
    all_to_all x2, blocking collectives, exchange(): lax.all_to_all(blocks, ('ctx', 'ch'), 0, 0, axis_index_groups=groups, til...  116 us
    pallas_call x3, Pallas kernels, call(): pl.pallas_call(kernel, out_shape=[(pltpu.VMEM if near else jax.ShapeDtype...  7.45 us

profile of v8, /device:TPU:1, one launch (start us, length us, event | category | flops | bytes accessed | tf_op | source)
XLA Modules:
  0.0 124.2 jit_solution(16376404971651468399)
XLA Ops:
  0.6 2.9 %shard_map.86 = f32[4608,128]{1,0:T(8,128)S(1)} custom-call(f32[4,256,256]{2,1,0:T(8,128)} %cotangent.1, f32[256,256]{1,0:T(8,128)} %filters.1, f32[4,256,256]{2,1,0:T(8,128)} %inputs.1), custom_call_target="tpu_custom_call" | custom-call | flops 1000000000 | bytes 4718592 | tf_op jit(solution)/shard_map/pallas_call | solution.py:264
  3.5 0.0 copy-start
  3.5 0.0 copy-start.1
  3.6 0.0 copy-start.2
  3.6 0.0 copy-start.3
  3.6 72.5 %all_to_all.10 = f32[128,9,4,128]{3,2,1,0:T(4,128)S(1)} all-to-all(f32[128,9,4,128]{3,2,1,0:T(4,128)S(1)} %bitcast.4), channel_id=1, replica_groups={{0,3,4,7,8,11,12,15,16,19,20,23,24,27,28,31,32,35,36,39,40,43,44,47,48,..., dimensions={0} | all-to-all | bytes 4718592 | tf_op jit(solution)/shard_map/all_to_all | solution.py:277
  76.1 0.0 copy-done
  76.1 0.0 copy-done.1
  76.1 0.0 copy-done.2
  76.1 0.0 copy-done.3
  76.1 3.3 %shard_map.87 = f32[2560,128]{1,0:T(8,128)S(1)} custom-call(f32[4608,128]{1,0:T(8,128)S(1)} %bitcast.5, bf16[64,192]{1,0:T(8,128)(2,1)S(1)} %copy-done.3, bf16[64,192]{1,0:T(8,128)(2,1)S(1)} %copy-done.2, f32[4,32,256]{2,1,0:T(8,128)S(1)} %copy-done.1, bf16[3,768,256]{2,1,0:T(8,128)(2,1)S(1)} %copy-done), custom_call_target="tpu_custom_call" | custom-call | flops 8000000000 | bytes 5029888 | tf_op jit(solution)/shard_map/pallas_call | solution.py:264
  79.5 43.5 %all_to_all.11 = f32[128,5,4,128]{3,2,1,0:T(4,128)S(1)} all-to-all(f32[128,5,4,128]{3,2,1,0:T(4,128)S(1)} %bitcast.6), channel_id=1, replica_groups={{0,3,4,7,8,11,12,15,16,19,20,23,24,27,28,31,32,35,36,39,40,43,44,47,48,..., dimensions={0} | all-to-all | bytes 2621440 | tf_op jit(solution)/shard_map/all_to_all | solution.py:277
  123.0 1.2 shard_map.88
Async XLA Ops:
  3.5 72.6 %copy-start = (bf16[3,768,256]{2,1,0:T(8,128)(2,1)S(1)}, bf16[3,768,256]{2,1,0:T(8,128)(2,1)}, u32[]{:S(2)}) copy-start(bf16[3,768,256]{2,1,0:T(8,128)(2,1)} %constant.11.clone.table) | copy-start | bytes 3538948
  3.5 72.6 %copy-start.1 = (f32[4,32,256]{2,1,0:T(8,128)S(1)}, f32[4,32,256]{2,1,0:T(8,128)}, u32[]{:S(2)}) copy-start(f32[4,32,256]{2,1,0:T(8,128)} %constant.10.clone.twiddle) | copy-start | bytes 393220
  3.6 72.6 %copy-start.2 = (bf16[64,192]{1,0:T(8,128)(2,1)S(1)}, bf16[64,192]{1,0:T(8,128)(2,1)}, u32[]{:S(2)}) copy-start(bf16[64,192]{1,0:T(8,128)(2,1)} %constant.9.clone.back) | copy-start | bytes 73732
  3.6 72.6 %copy-start.3 = (bf16[64,192]{1,0:T(8,128)(2,1)S(1)}, bf16[64,192]{1,0:T(8,128)(2,1)}, u32[]{:S(2)}) copy-start(bf16[64,192]{1,0:T(8,128)(2,1)} %constant.8.clone.across) | copy-start | bytes 73732

commit v9 on v7

--- a/solution.py
+++ b/solution.py
@@ -18,7 +18,6 @@
 PERIOD = ACROSS * WIDTH
 HALF = ACROSS // 2
 FACTOR = 1.0 / (PERIOD * math.sqrt(2.0 * PERIOD))
-AHEAD = 7
 VMEM = 48 * 1024 * 1024
 PACK_VMEM = 56 * 1024 * 1024
 
@@ -89,21 +88,27 @@
 
 
 def pack_kernel(cotangent, filters, inputs, out, held, sems):
-    blocks = [cotangent.at[b] for b in range(4)] + [filters] + [inputs.at[b] for b in range(4)]
-    copies = [pltpu.make_async_copy(block, held.at[u], sems.at[u]) for u, block in enumerate(blocks)]
-    for copy in copies[:AHEAD]:
+    pieces = [((4,), filters, held.at[4])]
+    for base, source in ((0, cotangent), (5, inputs)):
+        for b in (0, 2):
+            pair = (base + b, base + b + 1)
+            pieces.append((pair, source.at[pl.ds(b, 2)], held.at[pl.ds(base + b, 2)]))
+    copies = [
+        pltpu.make_async_copy(source, target, sems.at[k])
+        for k, (_, source, target) in enumerate(pieces)
+    ]
+    for copy in copies:
         copy.start()
 
     def run(order):
-        for u, copy in enumerate(copies):
+        for copy, (units, _, _) in zip(copies, pieces):
             copy.wait()
-            if u + AHEAD < len(copies):
-                copies[u + AHEAD].start()
-            turned = order(held[u].T)
-            for k in range(4):
-                out[pl.ds(u * 4 + k, GROUP, stride=36), :] = turned[
-                    k // 2 * GROUP : (k // 2 + 1) * GROUP, k % 2 * 128 : (k % 2 + 1) * 128
-                ]
+            for u in units:
+                turned = order(held[u].T)
+                for k in range(4):
+                    out[pl.ds(u * 4 + k, GROUP, stride=36), :] = turned[
+                        k // 2 * GROUP : (k // 2 + 1) * GROUP, k % 2 * 128 : (k % 2 + 1) * 128
+                    ]
 
     both_halves(run)
 
@@ -287,7 +292,7 @@
     (packed,) = call(
         pack_kernel,
         [(GROUP * 36, 128)],
-        [pltpu.VMEM((9, WIDTH, WIDTH), F32), pltpu.SemaphoreType.DMA((9,))],
+        [pltpu.VMEM((9, WIDTH, WIDTH), F32), pltpu.SemaphoreType.DMA((5,))],
         10**9,
         cotangent, filters, inputs,
         in_specs=[far] * 3,

time: 125 us -> 124 us (level)
  no operation moved by 1% of the time
where the time goes in v9:
time: 124 us; the launch traced here: 123 us
  blocking collectives  116 us (94%)
  Pallas kernels  6.54 us (5%)
    all_to_all x2, blocking collectives, exchange(): lax.all_to_all(blocks, ('ctx', 'ch'), 0, 0, axis_index_groups=groups, til...  116 us
    pallas_call x3, Pallas kernels, call(): pl.pallas_call(kernel, out_shape=[(pltpu.VMEM if near else jax.ShapeDtype...  6.54 us

profile of v9, /device:TPU:1, one launch (start us, length us, event | category | flops | bytes accessed | tf_op | source)
XLA Modules:
  0.0 123.3 jit_solution(15934454442858313604)
XLA Ops:
  0.6 2.0 %shard_map.86 = f32[4608,128]{1,0:T(8,128)S(1)} custom-call(f32[4,256,256]{2,1,0:T(8,128)} %cotangent.1, f32[256,256]{1,0:T(8,128)} %filters.1, f32[4,256,256]{2,1,0:T(8,128)} %inputs.1), custom_call_target="tpu_custom_call" | custom-call | flops 1000000000 | bytes 4718592 | tf_op jit(solution)/shard_map/pallas_call | solution.py:271
  2.6 0.0 copy-start
  2.6 0.0 copy-start.1
  2.6 0.0 copy-start.2
  2.7 0.0 copy-start.3
  2.7 72.5 %all_to_all.10 = f32[128,9,4,128]{3,2,1,0:T(4,128)S(1)} all-to-all(f32[128,9,4,128]{3,2,1,0:T(4,128)S(1)} %bitcast.4), channel_id=1, replica_groups={{0,3,4,7,8,11,12,15,16,19,20,23,24,27,28,31,32,35,36,39,40,43,44,47,48,..., dimensions={0} | all-to-all | bytes 4718592 | tf_op jit(solution)/shard_map/all_to_all | solution.py:284
  75.2 0.0 copy-done
  75.2 0.0 copy-done.1
  75.2 0.0 copy-done.2
  75.2 0.0 copy-done.3
  75.2 3.3 %shard_map.87 = f32[2560,128]{1,0:T(8,128)S(1)} custom-call(f32[4608,128]{1,0:T(8,128)S(1)} %bitcast.5, bf16[64,192]{1,0:T(8,128)(2,1)S(1)} %copy-done.3, bf16[64,192]{1,0:T(8,128)(2,1)S(1)} %copy-done.2, f32[4,32,256]{2,1,0:T(8,128)S(1)} %copy-done.1, bf16[3,768,256]{2,1,0:T(8,128)(2,1)S(1)} %copy-done), custom_call_target="tpu_custom_call" | custom-call | flops 8000000000 | bytes 5029888 | tf_op jit(solution)/shard_map/pallas_call | solution.py:271
  78.5 43.5 %all_to_all.11 = f32[128,5,4,128]{3,2,1,0:T(4,128)S(1)} all-to-all(f32[128,5,4,128]{3,2,1,0:T(4,128)S(1)} %bitcast.6), channel_id=1, replica_groups={{0,3,4,7,8,11,12,15,16,19,20,23,24,27,28,31,32,35,36,39,40,43,44,47,48,..., dimensions={0} | all-to-all | bytes 2621440 | tf_op jit(solution)/shard_map/all_to_all | solution.py:284
  122.1 1.2 shard_map.88
Async XLA Ops:
  2.6 72.6 %copy-start = (bf16[3,768,256]{2,1,0:T(8,128)(2,1)S(1)}, bf16[3,768,256]{2,1,0:T(8,128)(2,1)}, u32[]{:S(2)}) copy-start(bf16[3,768,256]{2,1,0:T(8,128)(2,1)} %constant.11.clone.table) | copy-start | bytes 3538948
  2.6 72.6 %copy-start.1 = (f32[4,32,256]{2,1,0:T(8,128)S(1)}, f32[4,32,256]{2,1,0:T(8,128)}, u32[]{:S(2)}) copy-start(f32[4,32,256]{2,1,0:T(8,128)} %constant.10.clone.twiddle) | copy-start | bytes 393220
  2.6 72.5 %copy-start.2 = (bf16[64,192]{1,0:T(8,128)(2,1)S(1)}, bf16[64,192]{1,0:T(8,128)(2,1)}, u32[]{:S(2)}) copy-start(bf16[64,192]{1,0:T(8,128)(2,1)} %constant.9.clone.back) | copy-start | bytes 73732
  2.7 72.5 %copy-start.3 = (bf16[64,192]{1,0:T(8,128)(2,1)S(1)}, bf16[64,192]{1,0:T(8,128)(2,1)}, u32[]{:S(2)}) copy-start(bf16[64,192]{1,0:T(8,128)(2,1)} %constant.8.clone.across) | copy-start | bytes 73732

commit v10 on v9

--- a/solution.py
+++ b/solution.py
@@ -90,9 +90,8 @@
 def pack_kernel(cotangent, filters, inputs, out, held, sems):
     pieces = [((4,), filters, held.at[4])]
     for base, source in ((0, cotangent), (5, inputs)):
-        for b in (0, 2):
-            pair = (base + b, base + b + 1)
-            pieces.append((pair, source.at[pl.ds(b, 2)], held.at[pl.ds(base + b, 2)]))
+        units = tuple(range(base, base + 4))
+        pieces.append((units, source, held.at[pl.ds(base, 4)]))
     copies = [
         pltpu.make_async_copy(source, target, sems.at[k])
         for k, (_, source, target) in enumerate(pieces)
@@ -292,7 +291,7 @@
     (packed,) = call(
         pack_kernel,
         [(GROUP * 36, 128)],
-        [pltpu.VMEM((9, WIDTH, WIDTH), F32), pltpu.SemaphoreType.DMA((5,))],
+        [pltpu.VMEM((9, WIDTH, WIDTH), F32), pltpu.SemaphoreType.DMA((3,))],
         10**9,
         cotangent, filters, inputs,
         in_specs=[far] * 3,

time: 124 us -> 124 us (level)
  no operation moved by 1% of the time
where the time goes in v10:
time: 124 us; the launch traced here: 123 us
  blocking collectives  116 us (94%)
  Pallas kernels  6.57 us (5%)
    all_to_all x2, blocking collectives, exchange(): lax.all_to_all(blocks, ('ctx', 'ch'), 0, 0, axis_index_groups=groups, til...  116 us
    pallas_call x3, Pallas kernels, call(): pl.pallas_call(kernel, out_shape=[(pltpu.VMEM if near else jax.ShapeDtype...  6.57 us

profile of v10, /device:TPU:1, one launch (start us, length us, event | category | flops | bytes accessed | tf_op | source)
XLA Modules:
  0.0 123.3 jit_solution(2902677612554927744)
XLA Ops:
  0.6 2.0 %shard_map.86 = f32[4608,128]{1,0:T(8,128)S(1)} custom-call(f32[4,256,256]{2,1,0:T(8,128)} %cotangent.1, f32[256,256]{1,0:T(8,128)} %filters.1, f32[4,256,256]{2,1,0:T(8,128)} %inputs.1), custom_call_target="tpu_custom_call" | custom-call | flops 1000000000 | bytes 4718592 | tf_op jit(solution)/shard_map/pallas_call | solution.py:270
  2.7 0.0 copy-start
  2.7 0.0 copy-start.1
  2.7 0.0 copy-start.2
  2.7 0.0 copy-start.3
  2.7 72.5 %all_to_all.10 = f32[128,9,4,128]{3,2,1,0:T(4,128)S(1)} all-to-all(f32[128,9,4,128]{3,2,1,0:T(4,128)S(1)} %bitcast.4), channel_id=1, replica_groups={{0,3,4,7,8,11,12,15,16,19,20,23,24,27,28,31,32,35,36,39,40,43,44,47,48,..., dimensions={0} | all-to-all | bytes 4718592 | tf_op jit(solution)/shard_map/all_to_all | solution.py:283
  75.2 0.0 copy-done
  75.2 0.0 copy-done.1
  75.2 0.0 copy-done.2
  75.2 0.0 copy-done.3
  75.2 3.3 %shard_map.87 = f32[2560,128]{1,0:T(8,128)S(1)} custom-call(f32[4608,128]{1,0:T(8,128)S(1)} %bitcast.5, bf16[64,192]{1,0:T(8,128)(2,1)S(1)} %copy-done.3, bf16[64,192]{1,0:T(8,128)(2,1)S(1)} %copy-done.2, f32[4,32,256]{2,1,0:T(8,128)S(1)} %copy-done.1, bf16[3,768,256]{2,1,0:T(8,128)(2,1)S(1)} %copy-done), custom_call_target="tpu_custom_call" | custom-call | flops 8000000000 | bytes 5029888 | tf_op jit(solution)/shard_map/pallas_call | solution.py:270
  78.6 43.5 %all_to_all.11 = f32[128,5,4,128]{3,2,1,0:T(4,128)S(1)} all-to-all(f32[128,5,4,128]{3,2,1,0:T(4,128)S(1)} %bitcast.6), channel_id=1, replica_groups={{0,3,4,7,8,11,12,15,16,19,20,23,24,27,28,31,32,35,36,39,40,43,44,47,48,..., dimensions={0} | all-to-all | bytes 2621440 | tf_op jit(solution)/shard_map/all_to_all | solution.py:283
  122.1 1.2 shard_map.88
Async XLA Ops:
  2.7 72.6 %copy-start = (bf16[3,768,256]{2,1,0:T(8,128)(2,1)S(1)}, bf16[3,768,256]{2,1,0:T(8,128)(2,1)}, u32[]{:S(2)}) copy-start(bf16[3,768,256]{2,1,0:T(8,128)(2,1)} %constant.11.clone.table) | copy-start | bytes 3538948
  2.7 72.6 %copy-start.1 = (f32[4,32,256]{2,1,0:T(8,128)S(1)}, f32[4,32,256]{2,1,0:T(8,128)}, u32[]{:S(2)}) copy-start(f32[4,32,256]{2,1,0:T(8,128)} %constant.10.clone.twiddle) | copy-start | bytes 393220
  2.7 72.5 %copy-start.2 = (bf16[64,192]{1,0:T(8,128)(2,1)S(1)}, bf16[64,192]{1,0:T(8,128)(2,1)}, u32[]{:S(2)}) copy-start(bf16[64,192]{1,0:T(8,128)(2,1)} %constant.9.clone.back) | copy-start | bytes 73732
  2.7 72.5 %copy-start.3 = (bf16[64,192]{1,0:T(8,128)(2,1)S(1)}, bf16[64,192]{1,0:T(8,128)(2,1)}, u32[]{:S(2)}) copy-start(bf16[64,192]{1,0:T(8,128)(2,1)} %constant.8.clone.across) | copy-start | bytes 73732
